TPU v7x, 32 devices: a whole 2x2x4 slice. The times are simulated.
32 devices in a mesh: shot: 2 (over y), gx: 4 (over z), gy: 2 (over x), gz: 2 (over core).
Axes of the slice: x: 2, y: 2, z: 4, core: 2. Of those that a mesh axis runs over, the one named last changes fastest.
Arguments:
- source_prev: float32 [96, 8, 1024], P(('shot', 'gx'), 'gy', 'gz'), parts along dimension 0, may hold values from -6 to 6
- source_now: float32 [96, 8, 1024], P(('shot', 'gx'), 'gy', 'gz'), parts along dimension 0, may hold values from -6 to 6
- receiver_prev: float32 [96, 8, 1024], P(('shot', 'gx'), 'gy', 'gz'), parts along dimension 0, may hold values from -6 to 6
- receiver_now: float32 [96, 8, 1024], P(('shot', 'gx'), 'gy', 'gz'), parts along dimension 0, may hold values from -6 to 6
- courant: float32 [48, 8, 1024], P('gx', 'gy', 'gz'), may hold values from 0.04 to 0.16
- absorbing: int32 [48, 8, 1024], P('gx', 'gy', 'gz'), may hold values from 0 to 8, as said below
- source_cell: int32 [6], P('shot'), parts along dimension 0, may hold values from 0 to 1023, as said below
- wavelet: float32 [8], P('shot'), parts along dimension 0, may hold values from -4 to 4
- receiver_cells: int32 [256, 2], P('shot'), parts along dimension 0, may hold values from 0 to 47, as said below
- traces: float32 [4, 256], P(None, 'shot'), parts along dimension 1, may hold values from -6 to 6
Outputs:
- source_field: float32 [96, 8, 1024], P(('shot', 'gx'), 'gy', 'gz'), parts along dimension 0
- receiver_field: float32 [96, 8, 1024], P(('shot', 'gx'), 'gy', 'gz'), parts along dimension 0
- filtered_image: bfloat16 [16, 96, 8, 1024], P(None, ('shot', 'gx'), 'gy', 'gz'), parts along dimension 1
There are 2 independent parts, one for each index of `shot`. A program takes and returns all parts, laid end to end along the dimension named above; an argument that names none is the same for every part. Nothing has to cross between parts.
Inputs may be any that keep to these rules, and one draw needn't show every extreme that they name: `source_cell`: the source's cell as (x, y, z), each coordinate within the grid. `receiver_cells`: each row is a receiver's (x, y) within the grid, on the top surface at depth 0; several receivers may share a cell. Depth of a cell into the absorbing layers along the four side faces and the bottom face, largest at the grid's faces; 0 in the interior; the top face has no layer.
All inputs are finite; a program needn't handle non-finite values.
Results may differ from a plain program's by a relative error of at most 0.001.
Values sent between devices are 32-bit elements; how exact they have to be, the bound alone decides.
A program may use at most 64 MiB of HBM per device.

v0:
```python
import jax
import jax.numpy as jnp
from jax import lax
from jax.sharding import PartitionSpec as P

LAGS = 16
STEPS = 4
EVERY = 2


stencil_weights = (8.0 / 5.0, -1.0 / 5.0, 8.0 / 315.0, -1.0 / 560.0)
centre_weight = -205.0 / 72.0


def with_halo(array, sides, width):
    for axis, dim in sides:
        size, length = (lax.axis_size(axis), array.shape[dim])
        up = [(i, (i + 1) % size) for i in range(size - 1)]
        down = [(j, i) for i, j in up]
        last = lax.slice_in_dim(array, length - width, length, axis=dim)
        first = lax.slice_in_dim(array, 0, width, axis=dim)
        before = lax.ppermute(last, axis, up)
        after = lax.ppermute(first, axis, down)
        array = jnp.concatenate([before, array, after], axis=dim)
    return array


def stencil(padded):
    size_x = padded.shape[-3] - 8
    size_y = padded.shape[-2] - 8
    size_z = padded.shape[-1] - 8

    def window(start_x, start_y, start_z):
        return padded[
            ..., start_x : start_x + size_x, start_y : start_y + size_y, start_z : start_z + size_z
        ]

    total = 3.0 * centre_weight * window(4, 4, 4)
    for reach, weight in enumerate(stencil_weights, 1):
        total = total + weight * (
            window(4 + reach, 4, 4)
            + window(4 - reach, 4, 4)
            + window(4, 4 + reach, 4)
            + window(4, 4 - reach, 4)
            + window(4, 4, 4 + reach)
            + window(4, 4, 4 - reach)
        )
    return total


def advance(padded, current, earlier, courant, damping):
    return (2.0 * current - (1.0 - damping) * earlier + courant * stencil(padded)) / (1.0 + damping)


def laplace(padded):
    size_x = padded.shape[-3] - 2
    size_y = padded.shape[-2] - 2
    size_z = padded.shape[-1] - 2

    def window(start_x, start_y, start_z):
        return padded[
            ..., start_x : start_x + size_x, start_y : start_y + size_y, start_z : start_z + size_z
        ]

    return 6.0 * window(1, 1, 1) - (
        window(2, 1, 1)
        + window(0, 1, 1)
        + window(1, 2, 1)
        + window(1, 0, 1)
        + window(1, 1, 2)
        + window(1, 1, 0)
    )


def correlate(widened, length):
    return jnp.stack(
        [
            widened[0, LAGS - offset : LAGS - offset + length]
            * widened[1, offset : offset + length]
            for offset in range(LAGS)
        ]
    )


def local(
    source_prev,
    source_now,
    receiver_prev,
    receiver_now,
    courant,
    absorbing,
    source_cell,
    wavelet,
    receiver_cells,
    traces,
):
    earlier = jnp.stack([source_prev, receiver_prev])
    current = jnp.stack([source_now, receiver_now])
    damping = absorbing.astype(jnp.float32) / 16.0
    tile_x, tile_y, tile_z = courant.shape
    x_anchor = lax.axis_index("gx") * tile_x
    y_cells = jnp.arange(tile_y, dtype=jnp.int32) + lax.axis_index("gy") * tile_y
    z_cells = jnp.arange(tile_z, dtype=jnp.int32) + lax.axis_index("gz") * tile_z
    surface = (lax.axis_index("gz") == 0).astype(jnp.float32)
    image = None
    x_cells = jnp.arange(tile_x, dtype=jnp.int32) + x_anchor
    for step_index in range(STEPS):
        padded = with_halo(current, (("gx", 1), ("gy", 2), ("gz", 3)), 4)
        upcoming = advance(padded, current, earlier, courant, damping)
        inject_upcoming = upcoming
        hit_x = (x_cells == source_cell[0]).astype(jnp.float32)
        hit_y = (y_cells == source_cell[1]).astype(jnp.float32)
        hit_z = (z_cells == source_cell[2]).astype(jnp.float32)
        point = hit_x[:, None, None] * hit_y[None, :, None] * hit_z[None, None, :]
        match_x = (receiver_cells[:, 0:1] == x_cells[None, :]).astype(jnp.float32) * traces[
            step_index
        ][:, None]
        match_y = (receiver_cells[:, 1:2] == y_cells[None, :]).astype(jnp.float32)
        sheet = jnp.einsum("rx,ry->xy", match_x, match_y, precision=lax.Precision.HIGHEST) * surface
        inject_upcoming = inject_upcoming.at[0].add(point * wavelet[step_index])
        upcoming = inject_upcoming.at[1, :, :, 0].add(sheet)
        earlier, current = (current, upcoming)
        if (step_index + 1) % EVERY == 0:
            widened = with_halo(current, (("gx", 1),), LAGS // 2)
            term = correlate(widened, tile_x)
            image = term if image is None else image + term
    framed = with_halo(image, (("gx", 1), ("gy", 2), ("gz", 3)), 1)
    filtered_image = laplace(framed).astype(jnp.bfloat16)
    return (current[0], current[1], filtered_image)


def solution(mesh):
    placed = (
        P(("shot", "gx"), "gy", "gz"),
        P(("shot", "gx"), "gy", "gz"),
        P(("shot", "gx"), "gy", "gz"),
        P(("shot", "gx"), "gy", "gz"),
        P("gx", "gy", "gz"),
        P("gx", "gy", "gz"),
        P("shot"),
        P("shot"),
        P("shot", None),
        P(None, "shot"),
    )
    return jax.shard_map(
        local,
        mesh=mesh,
        in_specs=placed,
        out_specs=(
            P(("shot", "gx"), "gy", "gz"),
            P(("shot", "gx"), "gy", "gz"),
            P(None, ("shot", "gx"), "gy", "gz"),
        ),
        check_vma=False,
    )
```

profile of v0, /device:TPU:0, one launch (start us, length us, event | category | flops | bytes accessed | tf_op | source)
XLA Modules:
  0.0 198.7 jit_solution(17501009136352425345)
XLA Ops:
  1.5 1.3 collective-permute-start
  2.8 5.6 %collective-permute-start.1 = (f32[2,4,4,512]{3,2,1,0:T(4,128)S(1)}, f32[2,4,4,512]{3,2,1,0:T(4,128)S(1)}, u32[]{:S(2)}, u32[]{:S(2)}) collective-permute-start(f32[2,4,4,512]{3,2,1,0:T(4,128)S(1)} %get-tuple-element.225), channel_id=1, source_target_pairs={{0,4},{4,8},{8,12},{1,5},{5,9},{9,13},{2,6},{6,10},{10,14},{3,7},{... | collective-permute-start | bytes 196616 | tf_op jit(solution)/shard_map/ppermute | solution.py:22
  8.3 1.4 fusion.271
  13.1 1.5 fusion.270
  15.6 3.9 %collective-permute-start.3 = (f32[2,20,4,512]{3,2,1,0:T(4,128)S(1)}, f32[2,20,4,512]{3,2,1,0:T(4,128)S(1)}, u32[]{:S(2)}, u32[]{:S(2)}) collective-permute-start(f32[2,20,4,512]{3,2,1,0:T(4,128)S(1)} %pad_maximum_fusion.26), channel_id=1, source_target_pairs={{0,2},{1,3},{4,6},{5,7},{8,10},{9,11},{12,14},{13,15},{16,18},{17,... | collective-permute-start | bytes 983048 | tf_op jit(solution)/shard_map/ppermute | solution.py:22
  21.1 1.3 collective-permute-start.2
  22.4 3.4 %collective-permute-done.3 = f32[2,20,4,512]{3,2,1,0:T(4,128)S(1)} collective-permute-done((f32[2,20,4,512]{3,2,1,0:T(4,128)S(1)}, f32[2,20,4,512]{3,2,1,0:T(4,128)S(1)}, u32[]{:S(2)}, u32[]{:S(2)}) %collective-permute-start.3) | collective-permute-done | bytes 327712 | tf_op jit(solution)/shard_map/ppermute | solution.py:22
  26.4 5.2 %collective-permute-done.2 = f32[2,20,4,512]{3,2,1,0:T(4,128)S(1)} collective-permute-done((f32[2,20,4,512]{3,2,1,0:T(4,128)S(1)}, f32[2,20,4,512]{3,2,1,0:T(4,128)S(1)}, u32[]{:S(2)}, u32[]{:S(2)}) %collective-permute-start.2) | collective-permute-done | bytes 327712 | tf_op jit(solution)/shard_map/ppermute | solution.py:23
  32.2 1.3 collective-permute-start.4
  33.5 3.1 %collective-permute-start.5 = (f32[2,20,12,4]{3,0,2,1:T(2,128)S(1)}, f32[2,20,12,4]{3,0,2,1:T(2,128)S(1)}, u32[]{:S(2)}, u32[]{:S(2)}) collective-permute-start(f32[2,20,12,4]{3,0,2,1:T(2,128)S(1)} %get-tuple-element.178), channel_id=1, source_target_pairs={{0,1},{2,3},{4,5},{6,7},{8,9},{10,11},{12,13},{14,15},{16,17},{18,... | collective-permute-start | bytes 23048 | tf_op jit(solution)/shard_map/ppermute | solution.py:22
  37.7 2.0 %pad_maximum_fusion.95 = (f32[2,12,4,512]{3,0,2,1:T(2,128)S(1)}, f32[2,12,4,512]{3,0,2,1:T(2,128)S(1)}, f32[2,12,4,512]{3,0,2,1:T(2,128)S(1)}, f32[2,12,4,512]{3...) fusion(f32[2,20,12,4]{3,0,2,1:T(2,128)S(1)} %collective-permute, ...), kind=kLoop, calls=%fused_computation.405 | loop fusion | flops 393216 | bytes 2571264 | tf_op jit(solution)/shard_map/slice | solution.py:34
  41.8 1.3 collective-permute-start.6
  43.1 4.6 %collective-permute-start.7 = (f32[2,4,4,512]{3,2,1,0:T(4,128)S(1)}, f32[2,4,4,512]{3,2,1,0:T(4,128)S(1)}, u32[]{:S(2)}, u32[]{:S(2)}) collective-permute-start(f32[2,4,4,512]{3,2,1,0:T(4,128)S(1)} %get-tuple-element.221), channel_id=1, source_target_pairs={{0,4},{4,8},{8,12},{1,5},{5,9},{9,13},{2,6},{6,10},{10,14},{3,7},{... | collective-permute-start | bytes 196616 | tf_op jit(solution)/shard_map/ppermute | solution.py:22
  48.1 1.5 collective-permute-done.7
  49.6 1.5 collective-permute-start.9
  51.1 1.3 collective-permute-start.8
  52.4 5.1 %collective-permute-done.9 = f32[2,20,4,512]{3,2,1,0:T(4,128)S(1)} collective-permute-done((f32[2,20,4,512]{3,2,1,0:T(4,128)S(1)}, f32[2,20,4,512]{3,2,1,0:T(4,128)S(1)}, u32[]{:S(2)}, u32[]{:S(2)}) %collective-permute-start.9) | collective-permute-done | bytes 327712 | tf_op jit(solution)/shard_map/ppermute | solution.py:22
  58.1 3.6 %collective-permute-done.8 = f32[2,20,4,512]{3,2,1,0:T(4,128)S(1)} collective-permute-done((f32[2,20,4,512]{3,2,1,0:T(4,128)S(1)}, f32[2,20,4,512]{3,2,1,0:T(4,128)S(1)}, u32[]{:S(2)}, u32[]{:S(2)}) %collective-permute-start.8) | collective-permute-done | bytes 327712 | tf_op jit(solution)/shard_map/ppermute | solution.py:23
  64.3 3.1 %collective-permute-start.11 = (f32[2,20,12,4]{3,0,2,1:T(2,128)S(1)}, f32[2,20,12,4]{3,0,2,1:T(2,128)S(1)}, u32[]{:S(2)}, u32[]{:S(2)}) collective-permute-start(f32[2,20,12,4]{3,0,2,1:T(2,128)S(1)} %get-tuple-element.172), channel_id=1, source_target_pairs={{0,1},{2,3},{4,5},{6,7},{8,9},{10,11},{12,13},{14,15},{16,17},{18,... | collective-permute-start | bytes 23048 | tf_op jit(solution)/shard_map/ppermute | solution.py:22
  68.4 2.0 %pad_maximum_fusion.79 = (f32[2,12,4,512]{3,0,2,1:T(2,128)S(1)}, f32[2,12,4,512]{3,0,2,1:T(2,128)S(1)}, f32[2,12,4,512]{3,0,2,1:T(2,128)S(1)}, f32[2,12,4,512]{3...) fusion(f32[2,20,12,4]{3,0,2,1:T(2,128)S(1)} %collective-permute, ...), kind=kLoop, calls=%fused_computation.365 | loop fusion | flops 393216 | bytes 2571264 | tf_op jit(solution)/shard_map/slice | solution.py:34
  73.9 4.6 %collective-permute-start.13 = (f32[2,4,4,512]{3,2,1,0:T(4,128)S(1)}, f32[2,4,4,512]{3,2,1,0:T(4,128)S(1)}, u32[]{:S(2)}, u32[]{:S(2)}) collective-permute-start(f32[2,4,4,512]{3,2,1,0:T(4,128)S(1)} %get-tuple-element.219), channel_id=1, source_target_pairs={{0,4},{4,8},{8,12},{1,5},{5,9},{9,13},{2,6},{6,10},{10,14},{3,7},{... | collective-permute-start | bytes 196616 | tf_op jit(solution)/shard_map/ppermute | solution.py:22
  80.5 1.5 collective-permute-start.15
  83.3 5.4 %collective-permute-done.15 = f32[2,20,4,512]{3,2,1,0:T(4,128)S(1)} collective-permute-done((f32[2,20,4,512]{3,2,1,0:T(4,128)S(1)}, f32[2,20,4,512]{3,2,1,0:T(4,128)S(1)}, u32[]{:S(2)}, u32[]{:S(2)}) %collective-permute-start.15) | collective-permute-done | bytes 327712 | tf_op jit(solution)/shard_map/ppermute | solution.py:22
  89.2 3.6 %collective-permute-done.14 = f32[2,20,4,512]{3,2,1,0:T(4,128)S(1)} collective-permute-done((f32[2,20,4,512]{3,2,1,0:T(4,128)S(1)}, f32[2,20,4,512]{3,2,1,0:T(4,128)S(1)}, u32[]{:S(2)}, u32[]{:S(2)}) %collective-permute-start.14) | collective-permute-done | bytes 327712 | tf_op jit(solution)/shard_map/ppermute | solution.py:23
  95.4 3.2 %collective-permute-start.17 = (f32[2,20,12,4]{3,0,2,1:T(2,128)S(1)}, f32[2,20,12,4]{3,0,2,1:T(2,128)S(1)}, u32[]{:S(2)}, u32[]{:S(2)}) collective-permute-start(f32[2,20,12,4]{3,0,2,1:T(2,128)S(1)} %get-tuple-element.166), channel_id=1, source_target_pairs={{0,1},{2,3},{4,5},{6,7},{8,9},{10,11},{12,13},{14,15},{16,17},{18,... | collective-permute-start | bytes 23048 | tf_op jit(solution)/shard_map/ppermute | solution.py:22
  99.6 2.0 %pad_maximum_fusion.63 = (f32[2,12,4,512]{3,0,2,1:T(2,128)S(1)}, f32[2,12,4,512]{3,0,2,1:T(2,128)S(1)}, f32[2,12,4,512]{3,0,2,1:T(2,128)S(1)}, f32[2,12,4,512]{3...) fusion(f32[2,20,12,4]{3,0,2,1:T(2,128)S(1)} %collective-permute, ...), kind=kLoop, calls=%fused_computation.343 | loop fusion | flops 393216 | bytes 2571264 | tf_op jit(solution)/shard_map/slice | solution.py:34
  105.0 5.1 %collective-permute-start.19 = (f32[2,4,4,512]{3,2,1,0:T(4,128)S(1)}, f32[2,4,4,512]{3,2,1,0:T(4,128)S(1)}, u32[]{:S(2)}, u32[]{:S(2)}) collective-permute-start(f32[2,4,4,512]{3,2,1,0:T(4,128)S(1)} %get-tuple-element.217), channel_id=1, source_target_pairs={{0,4},{4,8},{8,12},{1,5},{5,9},{9,13},{2,6},{6,10},{10,14},{3,7},{... | collective-permute-start | bytes 196616 | tf_op jit(solution)/shard_map/ppermute | solution.py:22
  111.5 4.6 %collective-permute-start.25 = (f32[2,8,4,512]{3,1,2,0:T(8,128)S(1)}, f32[2,8,4,512]{3,1,2,0:T(8,128)S(1)}, u32[]{:S(2)}, u32[]{:S(2)}) collective-permute-start(f32[2,8,4,512]{3,1,2,0:T(8,128)S(1)} %copy.954), channel_id=1, source_target_pairs={{0,4},{4,8},{8,12},{1,5},{5,9},{9,13},{2,6},{6,10},{10,14},{3,7},{... | collective-permute-start | bytes 393224 | tf_op jit(solution)/shard_map/ppermute | solution.py:22
  116.1 1.5 collective-permute-start.21
  118.9 1.3 collective-permute-start.20
  120.2 4.1 %collective-permute-done.21 = f32[2,20,4,512]{3,2,1,0:T(4,128)S(1)} collective-permute-done((f32[2,20,4,512]{3,2,1,0:T(4,128)S(1)}, f32[2,20,4,512]{3,2,1,0:T(4,128)S(1)}, u32[]{:S(2)}, u32[]{:S(2)}) %collective-permute-start.21) | collective-permute-done | bytes 327712 | tf_op jit(solution)/shard_map/ppermute | solution.py:22
  124.9 4.3 %collective-permute-done.20 = f32[2,20,4,512]{3,2,1,0:T(4,128)S(1)} collective-permute-done((f32[2,20,4,512]{3,2,1,0:T(4,128)S(1)}, f32[2,20,4,512]{3,2,1,0:T(4,128)S(1)}, u32[]{:S(2)}, u32[]{:S(2)}) %collective-permute-start.20) | collective-permute-done | bytes 327712 | tf_op jit(solution)/shard_map/ppermute | solution.py:23
  129.8 1.3 collective-permute-start.22
  131.1 3.1 %collective-permute-start.23 = (f32[2,20,12,4]{3,0,2,1:T(2,128)S(1)}, f32[2,20,12,4]{3,0,2,1:T(2,128)S(1)}, u32[]{:S(2)}, u32[]{:S(2)}) collective-permute-start(f32[2,20,12,4]{3,0,2,1:T(2,128)S(1)} %get-tuple-element.160), channel_id=1, source_target_pairs={{0,1},{2,3},{4,5},{6,7},{8,9},{10,11},{12,13},{14,15},{16,17},{18,... | collective-permute-start | bytes 23048 | tf_op jit(solution)/shard_map/ppermute | solution.py:22
  135.3 2.0 %pad_maximum_fusion.47 = (f32[2,12,4,512]{3,0,2,1:T(2,128)S(1)}, f32[2,12,4,512]{3,0,2,1:T(2,128)S(1)}, f32[2,12,4,512]{3,0,2,1:T(2,128)S(1)}, f32[2,12,4,512]{3...) fusion(f32[2,20,12,4]{3,0,2,1:T(2,128)S(1)} %collective-permute, ...), kind=kLoop, calls=%fused_computation.321 | loop fusion | flops 393216 | bytes 2571264 | tf_op jit(solution)/shard_map/slice | solution.py:34
  140.1 5.2 %collective-permute-start.27 = (f32[2,8,4,512]{3,1,2,0:T(8,128)}, f32[2,8,4,512]{3,1,2,0:T(8,128)}, u32[]{:S(2)}, u32[]{:S(2)}) collective-permute-start(f32[2,8,4,512]{3,1,2,0:T(8,128)} %copy.974), channel_id=1, source_target_pairs={{0,4},{4,8},{8,12},{1,5},{5,9},{9,13},{2,6},{6,10},{10,14},{3,7},{... | collective-permute-start | bytes 393224 | tf_op jit(solution)/shard_map/ppermute | solution.py:22
  146.0 1.5 collective-permute-start.26
  149.4 2.4 %stack.22 = f32[16,12,4,512]{3,0,2,1:T(8,128)S(1)} concatenate(f32[1,12,4,512]{3,0,2,1:T(1,128)S(1)} %copy.956, f32[1,12,4,512]{3,0,2,1:T(1,128)S(1)} %copy.957, f32[1,12,4,512]{3,0,2,1:T(1,128)S(1)} %copy.958, f32[1,12,4,512]{3,0,2,1:T(1,128)S(1)} %copy.959, f32[1,12,4,512]{3,0,2,1:T(1,128)S(1)} %copy.960, f32[1,12,4,512]{3,0,2,1:T(1,128)S(1)} %copy.961, ...), dimensions={0} | concatenate | bytes 3145728 | tf_op jit(solution)/shard_map/stack | solution.py:76
  158.1 4.4 %stack.23 = f32[16,12,4,512]{3,0,2,1:T(8,128)} concatenate(f32[1,12,4,512]{3,0,2,1:T(1,128)S(1)} %copy.976, f32[1,12,4,512]{3,0,2,1:T(1,128)S(1)} %copy.977, f32[1,12,4,512]{3,0,2,1:T(1,128)S(1)} %copy.978, f32[1,12,4,512]{3,0,2,1:T(1,128)S(1)} %copy.979, f32[1,12,4,512]{3,0,2,1:T(1,128)S(1)} %copy.980, f32[1,12,4,512]{3,0,2,1:T(1,128)S(1)} %copy.981, ...), dimensions={0} | concatenate | bytes 3145728 | tf_op jit(solution)/shard_map/stack | solution.py:76
  162.5 1.8 add.533
  165.6 4.6 %collective-permute-start.29 = (f32[16,1,4,512]{3,0,2,1:T(8,128)S(1)}, f32[16,1,4,512]{3,0,2,1:T(8,128)S(1)}, u32[]{:S(2)}, u32[]{:S(2)}) collective-permute-start(f32[16,1,4,512]{3,0,2,1:T(8,128)S(1)} %get-tuple-element.121), channel_id=1, source_target_pairs={{0,4},{4,8},{8,12},{1,5},{5,9},{9,13},{2,6},{6,10},{10,14},{3,7},{... | collective-permute-start | bytes 393224 | tf_op jit(solution)/shard_map/ppermute | solution.py:22
  170.1 1.4 collective-permute-done.28
  174.1 4.6 %collective-permute-start.31 = (f32[16,14,1,512]{3,0,2,1:T(8,128)S(1)}, f32[16,14,1,512]{3,0,2,1:T(8,128)S(1)}, u32[]{:S(2)}, u32[]{:S(2)}) collective-permute-start(f32[16,14,1,512]{3,0,2,1:T(8,128)S(1)} %get-tuple-element.119), channel_id=1, source_target_pairs={{0,2},{1,3},{4,6},{5,7},{8,10},{9,11},{12,14},{13,15},{16,18},{17,... | collective-permute-start | bytes 1376264 | tf_op jit(solution)/shard_map/ppermute | solution.py:22
  178.7 7.2 %collective-permute-done.30 = f32[16,14,1,512]{3,0,2,1:T(8,128)S(1)} collective-permute-done((f32[16,14,1,512]{3,0,2,1:T(8,128)S(1)}, f32[16,14,1,512]{3,0,2,1:T(8,128)S(1)}, u32[]{:S(2)}, u32[]{:S(2)}) %collective-permute-start.30) | collective-permute-done | bytes 458784 | tf_op jit(solution)/shard_map/ppermute | solution.py:23
  188.4 1.3 collective-permute-start.33
  190.2 1.3 collective-permute-start.32
  193.9 3.3 %fusion.2 = bf16[16,12,4,512]{3,0,2,1:T(8,128)(2,1)S(1)} fusion(f32[16,14,6,1]{3,0,2,1:T(8,128)S(1)} %copy.995, f32[16,14,1,512]{3,0,2,1:T(8,128)} %copy-done.2, f32[16,14,1,512]{3,0,2,1:T(8,128)} %copy-done.3, f32[16,1,4,512]{3,0,2,1:T(8,128)S(1)} %collective-permute-done.28, f32[16,12,4,512]{3,0,2,1:T(8,128)S(1)} %add.533, ...), kind=kLoop, calls=%fused_computation.3 | loop fusion | flops 10223616 | bytes 3549696 | tf_op jit(solution)/shard_map/convert_element_type | solution.py:128
  197.2 1.5 copy.996
  (160 shorter events, 55.3 us)
Async XLA Ops:
  1.5 13.1 %collective-permute-start = (f32[2,4,4,512]{3,2,1,0:T(4,128)S(1)}, f32[2,4,4,512]{3,2,1,0:T(4,128)S(1)}, u32[]{:S(2)}, u32[]{:S(2)}) collective-permute-start(f32[2,4,4,512]{3,2,1,0:T(4,128)S(1)} %get-tuple-element.226), channel_id=1, source_target_pairs={{4,0},{8,4},{12,8},{5,1},{9,5},{13,9},{6,2},{10,6},{14,10},{7,3},{... | collective-permute-start | bytes 196616 | tf_op jit(solution)/shard_map/ppermute | solution.py:23
  2.8 11.8 %collective-permute-start.1 = (f32[2,4,4,512]{3,2,1,0:T(4,128)S(1)}, f32[2,4,4,512]{3,2,1,0:T(4,128)S(1)}, u32[]{:S(2)}, u32[]{:S(2)}) collective-permute-start(f32[2,4,4,512]{3,2,1,0:T(4,128)S(1)} %get-tuple-element.225), channel_id=1, source_target_pairs={{0,4},{4,8},{8,12},{1,5},{5,9},{9,13},{2,6},{6,10},{10,14},{3,7},{... | collective-permute-start | bytes 196616 | tf_op jit(solution)/shard_map/ppermute | solution.py:22
  15.6 10.2 %collective-permute-start.3 = (f32[2,20,4,512]{3,2,1,0:T(4,128)S(1)}, f32[2,20,4,512]{3,2,1,0:T(4,128)S(1)}, u32[]{:S(2)}, u32[]{:S(2)}) collective-permute-start(f32[2,20,4,512]{3,2,1,0:T(4,128)S(1)} %pad_maximum_fusion.26), channel_id=1, source_target_pairs={{0,2},{1,3},{4,6},{5,7},{8,10},{9,11},{12,14},{13,15},{16,18},{17,... | collective-permute-start | bytes 983048 | tf_op jit(solution)/shard_map/ppermute | solution.py:22
  20.1 16.5 %copy-start = (f32[12,4,512]{2,1,0:T(4,128)S(1)}, f32[12,4,512]{2,1,0:T(4,128)}, u32[]{:S(2)}) copy-start(f32[12,4,512]{2,1,0:T(4,128)} %param.27) | copy-start | bytes 294916
  20.1 16.5 %copy-start.1 = (f32[12,4,512]{2,1,0:T(4,128)S(1)}, f32[12,4,512]{2,1,0:T(4,128)}, u32[]{:S(2)}) copy-start(f32[12,4,512]{2,1,0:T(4,128)} %param.29) | copy-start | bytes 294916
  21.1 10.5 %collective-permute-start.2 = (f32[2,20,4,512]{3,2,1,0:T(4,128)S(1)}, f32[2,20,4,512]{3,2,1,0:T(4,128)S(1)}, u32[]{:S(2)}, u32[]{:S(2)}) collective-permute-start(f32[2,20,4,512]{3,2,1,0:T(4,128)S(1)} %pad_maximum_fusion.26), channel_id=1, source_target_pairs={{2,0},{3,1},{6,4},{7,5},{10,8},{11,9},{14,12},{15,13},{18,16},{19,... | collective-permute-start | bytes 983048 | tf_op jit(solution)/shard_map/ppermute | solution.py:23
  32.2 4.5 %collective-permute-start.4 = (f32[2,20,12,4]{3,0,2,1:T(2,128)S(1)}, f32[2,20,12,4]{3,0,2,1:T(2,128)S(1)}, u32[]{:S(2)}, u32[]{:S(2)}) collective-permute-start(f32[2,20,12,4]{3,0,2,1:T(2,128)S(1)} %get-tuple-element.177), channel_id=1, source_target_pairs={{1,0},{3,2},{5,4},{7,6},{9,8},{11,10},{13,12},{15,14},{17,16},{19,... | collective-permute-start | bytes 23048 | tf_op jit(solution)/shard_map/ppermute | solution.py:23
  33.5 4.2 %collective-permute-start.5 = (f32[2,20,12,4]{3,0,2,1:T(2,128)S(1)}, f32[2,20,12,4]{3,0,2,1:T(2,128)S(1)}, u32[]{:S(2)}, u32[]{:S(2)}) collective-permute-start(f32[2,20,12,4]{3,0,2,1:T(2,128)S(1)} %get-tuple-element.178), channel_id=1, source_target_pairs={{0,1},{2,3},{4,5},{6,7},{8,9},{10,11},{12,13},{14,15},{16,17},{18,... | collective-permute-start | bytes 23048 | tf_op jit(solution)/shard_map/ppermute | solution.py:22
  36.7 3.0 %copy-start.4 = (f32[12,4,512]{2,1,0:T(4,128)S(1)}, f32[12,4,512]{2,1,0:T(4,128)}, u32[]{:S(2)}) copy-start(f32[12,4,512]{2,1,0:T(4,128)} %param.30) | copy-start | bytes 294916
  36.7 3.0 %copy-start.5 = (f32[12,4,512]{2,1,0:T(4,128)S(1)}, f32[12,4,512]{2,1,0:T(4,128)}, u32[]{:S(2)}) copy-start(f32[12,4,512]{2,1,0:T(4,128)} %param.28) | copy-start | bytes 294916
  36.7 3.0 %copy-start.6 = (f32[12,4,512]{2,1,0:T(4,128)S(1)}, f32[12,4,512]{2,1,0:T(4,128)}, u32[]{:S(2)}) copy-start(f32[12,4,512]{2,1,0:T(4,128)} %param.26) | copy-start | bytes 294916
  41.8 6.3 %collective-permute-start.6 = (f32[2,4,4,512]{3,2,1,0:T(4,128)S(1)}, f32[2,4,4,512]{3,2,1,0:T(4,128)S(1)}, u32[]{:S(2)}, u32[]{:S(2)}) collective-permute-start(f32[2,4,4,512]{3,2,1,0:T(4,128)S(1)} %get-tuple-element.222), channel_id=1, source_target_pairs={{4,0},{8,4},{12,8},{5,1},{9,5},{13,9},{6,2},{10,6},{14,10},{7,3},{... | collective-permute-start | bytes 196616 | tf_op jit(solution)/shard_map/ppermute | solution.py:23
  43.1 6.5 %collective-permute-start.7 = (f32[2,4,4,512]{3,2,1,0:T(4,128)S(1)}, f32[2,4,4,512]{3,2,1,0:T(4,128)S(1)}, u32[]{:S(2)}, u32[]{:S(2)}) collective-permute-start(f32[2,4,4,512]{3,2,1,0:T(4,128)S(1)} %get-tuple-element.221), channel_id=1, source_target_pairs={{0,4},{4,8},{8,12},{1,5},{5,9},{9,13},{2,6},{6,10},{10,14},{3,7},{... | collective-permute-start | bytes 196616 | tf_op jit(solution)/shard_map/ppermute | solution.py:22
  49.6 7.9 %collective-permute-start.9 = (f32[2,20,4,512]{3,2,1,0:T(4,128)S(1)}, f32[2,20,4,512]{3,2,1,0:T(4,128)S(1)}, u32[]{:S(2)}, u32[]{:S(2)}) collective-permute-start(f32[2,20,4,512]{3,2,1,0:T(4,128)S(1)} %pad_maximum_fusion.27), channel_id=1, source_target_pairs={{0,2},{1,3},{4,6},{5,7},{8,10},{9,11},{12,14},{13,15},{16,18},{17,... | collective-permute-start | bytes 983048 | tf_op jit(solution)/shard_map/ppermute | solution.py:22
  51.1 10.6 %collective-permute-start.8 = (f32[2,20,4,512]{3,2,1,0:T(4,128)S(1)}, f32[2,20,4,512]{3,2,1,0:T(4,128)S(1)}, u32[]{:S(2)}, u32[]{:S(2)}) collective-permute-start(f32[2,20,4,512]{3,2,1,0:T(4,128)S(1)} %pad_maximum_fusion.27), channel_id=1, source_target_pairs={{2,0},{3,1},{6,4},{7,5},{10,8},{11,9},{14,12},{15,13},{18,16},{19,... | collective-permute-start | bytes 983048 | tf_op jit(solution)/shard_map/ppermute | solution.py:23
  63.0 4.7 %collective-permute-start.10 = (f32[2,20,12,4]{3,0,2,1:T(2,128)}, f32[2,20,12,4]{3,0,2,1:T(2,128)S(1)}, u32[]{:S(2)}, u32[]{:S(2)}) collective-permute-start(f32[2,20,12,4]{3,0,2,1:T(2,128)} %get-tuple-element.171), channel_id=1, source_target_pairs={{1,0},{3,2},{5,4},{7,6},{9,8},{11,10},{13,12},{15,14},{17,16},{19,... | collective-permute-start | bytes 23048 | tf_op jit(solution)/shard_map/ppermute | solution.py:23
  64.3 4.2 %collective-permute-start.11 = (f32[2,20,12,4]{3,0,2,1:T(2,128)S(1)}, f32[2,20,12,4]{3,0,2,1:T(2,128)S(1)}, u32[]{:S(2)}, u32[]{:S(2)}) collective-permute-start(f32[2,20,12,4]{3,0,2,1:T(2,128)S(1)} %get-tuple-element.172), channel_id=1, source_target_pairs={{0,1},{2,3},{4,5},{6,7},{8,9},{10,11},{12,13},{14,15},{16,17},{18,... | collective-permute-start | bytes 23048 | tf_op jit(solution)/shard_map/ppermute | solution.py:22
  72.6 6.6 %collective-permute-start.12 = (f32[2,4,4,512]{3,2,1,0:T(4,128)S(1)}, f32[2,4,4,512]{3,2,1,0:T(4,128)S(1)}, u32[]{:S(2)}, u32[]{:S(2)}) collective-permute-start(f32[2,4,4,512]{3,2,1,0:T(4,128)S(1)} %get-tuple-element.220), channel_id=1, source_target_pairs={{4,0},{8,4},{12,8},{5,1},{9,5},{13,9},{6,2},{10,6},{14,10},{7,3},{... | collective-permute-start | bytes 196616 | tf_op jit(solution)/shard_map/ppermute | solution.py:23
  73.9 6.5 %collective-permute-start.13 = (f32[2,4,4,512]{3,2,1,0:T(4,128)S(1)}, f32[2,4,4,512]{3,2,1,0:T(4,128)S(1)}, u32[]{:S(2)}, u32[]{:S(2)}) collective-permute-start(f32[2,4,4,512]{3,2,1,0:T(4,128)S(1)} %get-tuple-element.219), channel_id=1, source_target_pairs={{0,4},{4,8},{8,12},{1,5},{5,9},{9,13},{2,6},{6,10},{10,14},{3,7},{... | collective-permute-start | bytes 196616 | tf_op jit(solution)/shard_map/ppermute | solution.py:22
  80.5 8.2 %collective-permute-start.15 = (f32[2,20,4,512]{3,2,1,0:T(4,128)S(1)}, f32[2,20,4,512]{3,2,1,0:T(4,128)S(1)}, u32[]{:S(2)}, u32[]{:S(2)}) collective-permute-start(f32[2,20,4,512]{3,2,1,0:T(4,128)S(1)} %pad_maximum_fusion.28), channel_id=1, source_target_pairs={{0,2},{1,3},{4,6},{5,7},{8,10},{9,11},{12,14},{13,15},{16,18},{17,... | collective-permute-start | bytes 983048 | tf_op jit(solution)/shard_map/ppermute | solution.py:22
  82.0 10.9 %collective-permute-start.14 = (f32[2,20,4,512]{3,2,1,0:T(4,128)S(1)}, f32[2,20,4,512]{3,2,1,0:T(4,128)S(1)}, u32[]{:S(2)}, u32[]{:S(2)}) collective-permute-start(f32[2,20,4,512]{3,2,1,0:T(4,128)S(1)} %pad_maximum_fusion.28), channel_id=1, source_target_pairs={{2,0},{3,1},{6,4},{7,5},{10,8},{11,9},{14,12},{15,13},{18,16},{19,... | collective-permute-start | bytes 983048 | tf_op jit(solution)/shard_map/ppermute | solution.py:23
  94.1 4.9 %collective-permute-start.16 = (f32[2,20,12,4]{3,0,2,1:T(2,128)}, f32[2,20,12,4]{3,0,2,1:T(2,128)S(1)}, u32[]{:S(2)}, u32[]{:S(2)}) collective-permute-start(f32[2,20,12,4]{3,0,2,1:T(2,128)} %get-tuple-element.165), channel_id=1, source_target_pairs={{1,0},{3,2},{5,4},{7,6},{9,8},{11,10},{13,12},{15,14},{17,16},{19,... | collective-permute-start | bytes 23048 | tf_op jit(solution)/shard_map/ppermute | solution.py:23
  95.4 4.2 %collective-permute-start.17 = (f32[2,20,12,4]{3,0,2,1:T(2,128)S(1)}, f32[2,20,12,4]{3,0,2,1:T(2,128)S(1)}, u32[]{:S(2)}, u32[]{:S(2)}) collective-permute-start(f32[2,20,12,4]{3,0,2,1:T(2,128)S(1)} %get-tuple-element.166), channel_id=1, source_target_pairs={{0,1},{2,3},{4,5},{6,7},{8,9},{10,11},{12,13},{14,15},{16,17},{18,... | collective-permute-start | bytes 23048 | tf_op jit(solution)/shard_map/ppermute | solution.py:22
  103.7 12.4 %collective-permute-start.18 = (f32[2,4,4,512]{3,2,1,0:T(4,128)S(1)}, f32[2,4,4,512]{3,2,1,0:T(4,128)S(1)}, u32[]{:S(2)}, u32[]{:S(2)}) collective-permute-start(f32[2,4,4,512]{3,2,1,0:T(4,128)S(1)} %get-tuple-element.218), channel_id=1, source_target_pairs={{4,0},{8,4},{12,8},{5,1},{9,5},{13,9},{6,2},{10,6},{14,10},{7,3},{... | collective-permute-start | bytes 196616 | tf_op jit(solution)/shard_map/ppermute | solution.py:23
  105.0 11.1 %collective-permute-start.19 = (f32[2,4,4,512]{3,2,1,0:T(4,128)S(1)}, f32[2,4,4,512]{3,2,1,0:T(4,128)S(1)}, u32[]{:S(2)}, u32[]{:S(2)}) collective-permute-start(f32[2,4,4,512]{3,2,1,0:T(4,128)S(1)} %get-tuple-element.217), channel_id=1, source_target_pairs={{0,4},{4,8},{8,12},{1,5},{5,9},{9,13},{2,6},{6,10},{10,14},{3,7},{... | collective-permute-start | bytes 196616 | tf_op jit(solution)/shard_map/ppermute | solution.py:22
  110.1 7.9 %collective-permute-start.24 = (f32[2,8,4,512]{3,1,2,0:T(8,128)S(1)}, f32[2,8,4,512]{3,1,2,0:T(8,128)S(1)}, u32[]{:S(2)}, u32[]{:S(2)}) collective-permute-start(f32[2,8,4,512]{3,1,2,0:T(8,128)S(1)} %copy.952), channel_id=1, source_target_pairs={{4,0},{8,4},{12,8},{5,1},{9,5},{13,9},{6,2},{10,6},{14,10},{7,3},{... | collective-permute-start | bytes 393224 | tf_op jit(solution)/shard_map/ppermute | solution.py:23
  111.5 7.3 %collective-permute-start.25 = (f32[2,8,4,512]{3,1,2,0:T(8,128)S(1)}, f32[2,8,4,512]{3,1,2,0:T(8,128)S(1)}, u32[]{:S(2)}, u32[]{:S(2)}) collective-permute-start(f32[2,8,4,512]{3,1,2,0:T(8,128)S(1)} %copy.954), channel_id=1, source_target_pairs={{0,4},{4,8},{8,12},{1,5},{5,9},{9,13},{2,6},{6,10},{10,14},{3,7},{... | collective-permute-start | bytes 393224 | tf_op jit(solution)/shard_map/ppermute | solution.py:22
  116.1 8.2 %collective-permute-start.21 = (f32[2,20,4,512]{3,2,1,0:T(4,128)S(1)}, f32[2,20,4,512]{3,2,1,0:T(4,128)S(1)}, u32[]{:S(2)}, u32[]{:S(2)}) collective-permute-start(f32[2,20,4,512]{3,2,1,0:T(4,128)S(1)} %pad_maximum_fusion.29), channel_id=1, source_target_pairs={{0,2},{1,3},{4,6},{5,7},{8,10},{9,11},{12,14},{13,15},{16,18},{17,... | collective-permute-start | bytes 983048 | tf_op jit(solution)/shard_map/ppermute | solution.py:22
  118.9 10.3 %collective-permute-start.20 = (f32[2,20,4,512]{3,2,1,0:T(4,128)S(1)}, f32[2,20,4,512]{3,2,1,0:T(4,128)S(1)}, u32[]{:S(2)}, u32[]{:S(2)}) collective-permute-start(f32[2,20,4,512]{3,2,1,0:T(4,128)S(1)} %pad_maximum_fusion.29), channel_id=1, source_target_pairs={{2,0},{3,1},{6,4},{7,5},{10,8},{11,9},{14,12},{15,13},{18,16},{19,... | collective-permute-start | bytes 983048 | tf_op jit(solution)/shard_map/ppermute | solution.py:23
  129.8 4.5 %collective-permute-start.22 = (f32[2,20,12,4]{3,0,2,1:T(2,128)S(1)}, f32[2,20,12,4]{3,0,2,1:T(2,128)S(1)}, u32[]{:S(2)}, u32[]{:S(2)}) collective-permute-start(f32[2,20,12,4]{3,0,2,1:T(2,128)S(1)} %get-tuple-element.159), channel_id=1, source_target_pairs={{1,0},{3,2},{5,4},{7,6},{9,8},{11,10},{13,12},{15,14},{17,16},{19,... | collective-permute-start | bytes 23048 | tf_op jit(solution)/shard_map/ppermute | solution.py:23
  131.1 4.2 %collective-permute-start.23 = (f32[2,20,12,4]{3,0,2,1:T(2,128)S(1)}, f32[2,20,12,4]{3,0,2,1:T(2,128)S(1)}, u32[]{:S(2)}, u32[]{:S(2)}) collective-permute-start(f32[2,20,12,4]{3,0,2,1:T(2,128)S(1)} %get-tuple-element.160), channel_id=1, source_target_pairs={{0,1},{2,3},{4,5},{6,7},{8,9},{10,11},{12,13},{14,15},{16,17},{18,... | collective-permute-start | bytes 23048 | tf_op jit(solution)/shard_map/ppermute | solution.py:22
  140.1 11.8 %collective-permute-start.27 = (f32[2,8,4,512]{3,1,2,0:T(8,128)}, f32[2,8,4,512]{3,1,2,0:T(8,128)}, u32[]{:S(2)}, u32[]{:S(2)}) collective-permute-start(f32[2,8,4,512]{3,1,2,0:T(8,128)} %copy.974), channel_id=1, source_target_pairs={{0,4},{4,8},{8,12},{1,5},{5,9},{9,13},{2,6},{6,10},{10,14},{3,7},{... | collective-permute-start | bytes 393224 | tf_op jit(solution)/shard_map/ppermute | solution.py:22
  146.0 7.7 %collective-permute-start.26 = (f32[2,8,4,512]{3,1,2,0:T(8,128)}, f32[2,8,4,512]{3,1,2,0:T(8,128)}, u32[]{:S(2)}, u32[]{:S(2)}) collective-permute-start(f32[2,8,4,512]{3,1,2,0:T(8,128)} %copy.972), channel_id=1, source_target_pairs={{4,0},{8,4},{12,8},{5,1},{9,5},{13,9},{6,2},{10,6},{14,10},{7,3},{... | collective-permute-start | bytes 393224 | tf_op jit(solution)/shard_map/ppermute | solution.py:23
  164.3 7.2 %collective-permute-start.28 = (f32[16,1,4,512]{3,0,2,1:T(8,128)S(1)}, f32[16,1,4,512]{3,0,2,1:T(8,128)S(1)}, u32[]{:S(2)}, u32[]{:S(2)}) collective-permute-start(f32[16,1,4,512]{3,0,2,1:T(8,128)S(1)} %get-tuple-element.122), channel_id=1, source_target_pairs={{4,0},{8,4},{12,8},{5,1},{9,5},{13,9},{6,2},{10,6},{14,10},{7,3},{... | collective-permute-start | bytes 393224 | tf_op jit(solution)/shard_map/ppermute | solution.py:23
  165.6 7.1 %collective-permute-start.29 = (f32[16,1,4,512]{3,0,2,1:T(8,128)S(1)}, f32[16,1,4,512]{3,0,2,1:T(8,128)S(1)}, u32[]{:S(2)}, u32[]{:S(2)}) collective-permute-start(f32[16,1,4,512]{3,0,2,1:T(8,128)S(1)} %get-tuple-element.121), channel_id=1, source_target_pairs={{0,4},{4,8},{8,12},{1,5},{5,9},{9,13},{2,6},{6,10},{10,14},{3,7},{... | collective-permute-start | bytes 393224 | tf_op jit(solution)/shard_map/ppermute | solution.py:22
  172.8 13.1 %collective-permute-start.30 = (f32[16,14,1,512]{3,0,2,1:T(8,128)S(1)}, f32[16,14,1,512]{3,0,2,1:T(8,128)S(1)}, u32[]{:S(2)}, u32[]{:S(2)}) collective-permute-start(f32[16,14,1,512]{3,0,2,1:T(8,128)S(1)} %get-tuple-element.120), channel_id=1, source_target_pairs={{2,0},{3,1},{6,4},{7,5},{10,8},{11,9},{14,12},{15,13},{18,16},{19,... | collective-permute-start | bytes 1376264 | tf_op jit(solution)/shard_map/ppermute | solution.py:23
  174.1 13.0 %collective-permute-start.31 = (f32[16,14,1,512]{3,0,2,1:T(8,128)S(1)}, f32[16,14,1,512]{3,0,2,1:T(8,128)S(1)}, u32[]{:S(2)}, u32[]{:S(2)}) collective-permute-start(f32[16,14,1,512]{3,0,2,1:T(8,128)S(1)} %get-tuple-element.119), channel_id=1, source_target_pairs={{0,2},{1,3},{4,6},{5,7},{8,10},{9,11},{12,14},{13,15},{16,18},{17,... | collective-permute-start | bytes 1376264 | tf_op jit(solution)/shard_map/ppermute | solution.py:22
  185.8 1.2 copy-start.2
  187.0 0.8 copy-start.3
  188.4 3.2 %collective-permute-start.33 = (f32[16,14,6,1]{0,3,2,1:T(1,128)S(1)}, f32[16,14,6,1]{0,3,2,1:T(1,128)S(1)}, u32[]{:S(2)}, u32[]{:S(2)}) collective-permute-start(f32[16,14,6,1]{0,3,2,1:T(1,128)S(1)} %copy.1030), channel_id=1, source_target_pairs={{0,1},{2,3},{4,5},{6,7},{8,9},{10,11},{12,13},{14,15},{16,17},{18,... | collective-permute-start | bytes 16136 | tf_op jit(solution)/shard_map/ppermute | solution.py:22
  190.2 3.1 %collective-permute-start.32 = (f32[16,14,6,1]{0,3,2,1:T(1,128)S(1)}, f32[16,14,6,1]{0,3,2,1:T(1,128)S(1)}, u32[]{:S(2)}, u32[]{:S(2)}) collective-permute-start(f32[16,14,6,1]{0,3,2,1:T(1,128)S(1)} %copy.1029), channel_id=1, source_target_pairs={{1,0},{3,2},{5,4},{7,6},{9,8},{11,10},{13,12},{15,14},{17,16},{19,... | collective-permute-start | bytes 16136 | tf_op jit(solution)/shard_map/ppermute | solution.py:23
where the time goes:
time: 201 us; the launch traced here: 199 us
  starting transfers between devices  82.8 us (41%)
  waiting for transfers between devices  55.4 us (28%)
  local copies, waits for them, and re-layouts  29.4 us (15%)
  other arithmetic  28.3 us (14%)
    ppermute x17, starting transfers between devices, with_halo(): before = lax.ppermute(last, axis, up)  60.7 us
    ppermute x17, waiting for transfers between devices, with_halo(): after = lax.ppermute(first, axis, down)  28.4 us
    ppermute x17, waiting for transfers between devices, with_halo(): before = lax.ppermute(last, axis, up)  27 us
    ppermute x17, starting transfers between devices, with_halo(): after = lax.ppermute(first, axis, down)  22.2 us
    slice x4, other arithmetic, window(): padded[..., start_x:start_x + size_x, start_y:start_y + size_y, start_z:s...  8.14 us
    another operation x2, local copies, waits for them, and re-layouts, correlate(): jnp.stack([widened[0, LAGS - offset:LAGS - offset + length] * widened[1,...  6.85 us
    unnamed x25, local copies, waits for them, and re-layouts  5.27 us
    div x4, other arithmetic, advance(): (2.0 * current - (1.0 - damping) * earlier + courant * stencil(padded)) /...  4.61 us
  transfers between devices with their start and end apart: 34, of which 23 were waited for; matrix products, arithmetic and copies ran while one was open for 9% of the time, Pallas kernels for 0%

commit v1 on v0

v1 whole, which is shorter than its diff:
```python
import functools
import jax
import jax.numpy as jnp
from jax import lax
from jax.experimental import pallas as pl
from jax.experimental.pallas import tpu as pltpu
from jax.sharding import PartitionSpec as P

LAGS = 16
STEPS = 4
EVERY = 2
HALF = LAGS // 2
H = HALF + 1
REACH = 4
LANES = 128

W1, W2, W3, W4 = (8.0 / 5.0, -1.0 / 5.0, 8.0 / 315.0, -1.0 / 560.0)
centre_weight = -205.0 / 72.0
MESH = pl.DeviceIdType.MESH


def kernel(
    sp, sn, rp, rn, cr, ab, cell, wav, rc, tr,
    out_s, out_r, out_i,
    F, YB, YC, ZL, ZR, PS, YPB, YPC, E, G, GE, D, DG, CA, CB, CC, INJ, IM, IH, LP, ST,
    send, recv,
):
    tx, ty, tz = sn.shape
    nchunk = tx // REACH
    nx, ny, nz = (lax.axis_size(a) for a in ("gx", "gy", "gz"))
    ix, iy, iz = (lax.axis_index(a) for a in ("gx", "gy", "gz"))
    copies = []

    def exists(dx, dy, dz):
        ok = None
        for d, i, n in ((dx, ix, nx), (dy, iy, ny), (dz, iz, nz)):
            if d:
                here = (i + d >= 0) & (i + d < n)
                ok = here if ok is None else ok & here
        return ok

    def device(dx, dy, dz):
        return {
            a: i + d for a, i, d in (("gx", ix, dx), ("gy", iy, dy), ("gz", iz, dz)) if d
        }

    class Copy:
        def __init__(self, src, dst, direction):
            number = len(copies)
            self.desc = pltpu.make_async_remote_copy(
                src_ref=src,
                dst_ref=dst,
                send_sem=send.at[number],
                recv_sem=recv.at[number],
                device_id=device(*direction),
                device_id_type=MESH,
            )
            self.out = exists(*direction)
            self.into = exists(*(-d for d in direction))
            copies.append(self)
            pl.when(self.out)(lambda: self.desc.start())

        def wait(self):
            pl.when(self.into)(lambda: self.desc.wait_recv())

        def finish(self):
            pl.when(self.out)(lambda: self.desc.wait_send())

    lane = lax.broadcasted_iota(jnp.int32, (8, LANES), 1)
    sub_z = lax.broadcasted_iota(jnp.int32, (8, tz), 0)
    lane_z = lax.broadcasted_iota(jnp.int32, (8, tz), 1)
    even, odd = pl.ds(0, ty, 2), pl.ds(1, ty, 2)

    def each(low, high, body, unroll=1):
        def step(i, carry):
            body(i)
            return carry

        lax.fori_loop(low, high, step, 0, unroll=unroll)

    tiles = tz // LANES

    def weave(slot, x, a, b):
        for q in range(tiles):
            part = slice(q * LANES, (q + 1) * LANES)
            ST[slot, x, q, even, :] = a[:, part]
            ST[slot, x, q, odd, :] = b[:, part]
        return jnp.concatenate([ST[slot, x, q] for q in range(tiles)], axis=1)

    def unweave(x, v, at):
        for q in range(tiles):
            LP[x, q] = v[:, q * LANES : (q + 1) * LANES]
        return [
            jnp.concatenate([LP[x, q, rows, :] for q in range(tiles)], axis=1) for rows in at
        ]

    def load_now(x):
        F[1, H + x] = weave(0, x, sn[x], rn[x])

    each(0, tx, load_now)

    low_x, high_x = ix == 0, ix == nx - 1
    low_y, high_y = iy == 0, iy == ny - 1
    low_z, high_z = iz == 0, iz == nz - 1

    @pl.when(low_x)
    def _():
        for i in range(1, STEPS + 2):
            F[i, 0:H] = jnp.zeros((H, 8, tz), jnp.float32)

    @pl.when(high_x)
    def _():
        for i in range(1, STEPS + 2):
            F[i, H + tx : 2 * H + tx] = jnp.zeros((H, 8, tz), jnp.float32)

    for missing, buf, packed in ((low_y, YB, YPB), (high_y, YC, YPC)):

        @pl.when(missing)
        def _(buf=buf):
            buf[...] = jnp.zeros(buf.shape, jnp.float32)

        @pl.when(missing | low_x | high_x)
        def _(packed=packed):
            packed[...] = jnp.zeros(packed.shape, jnp.float32)

    for missing, buf in ((low_z, ZL), (high_z, ZR)):

        @pl.when(missing | low_x | high_x)
        def _(buf=buf):
            buf[...] = jnp.zeros(buf.shape, jnp.float32)

    signs = (-1, 1)
    around = [(s, 0, 0) for s in signs] + [(0, s, 0) for s in signs] + [(0, 0, s) for s in signs]
    around += [(s, r, 0) for s in signs for r in signs] + [(s, 0, r) for s in signs for r in signs]
    barrier = pltpu.get_barrier_semaphore()
    count = 0
    for direction in around:
        there = exists(*direction)
        count = count + there.astype(jnp.int32)

        @pl.when(there)
        def _(direction=direction):
            pl.semaphore_signal(
                barrier, inc=1, device_id=device(*direction), device_id_type=MESH
            )

    pl.semaphore_wait(barrier, count)

    def send_x(f, low, high):
        left = Copy(
            F.at[f, H + low : H + high],
            F.at[f, H + tx + low : H + tx + high],
            (-1, 0, 0),
        )
        right = Copy(
            F.at[f, H + tx - high : H + tx - low],
            F.at[f, H - high : H - low],
            (1, 0, 0),
        )
        return left, right

    def send_y(f, c):
        own = F.at[f, H + c * REACH : H + (c + 1) * REACH]
        there = pl.ds(c * REACH, REACH)
        return (
            Copy(own, YB.at[f - 1, there], (0, 1, 0)),
            Copy(own, YC.at[f - 1, there], (0, -1, 0)),
        )

    def send_z(f, low, high, dx=0):
        rows = pl.ds(H + low, high - low)
        there = pl.ds(H + low - dx * tx, high - low)
        return (
            Copy(F.at[f, rows, :, pl.ds(tz - LANES, LANES)], ZL.at[f - 1, there], (dx, 0, 1)),
            Copy(F.at[f, rows, :, pl.ds(0, LANES)], ZR.at[f - 1, there], (dx, 0, -1)),
        )

    def send_rows(f, s):
        def pack(g):
            first, last = F[f, H + g * REACH], F[f, H + g * REACH]
            last = pltpu.roll(last, 2, 0)
            for j in range(1, REACH):
                row = F[f, H + g * REACH + j]
                here = sub_z // 2 == j
                first = jnp.where(here, pltpu.roll(row, 2 * j, 0), first)
                shift = (2 * j - 6) % 8
                last = jnp.where(here, pltpu.roll(row, shift, 0) if shift else row, last)
            PS[s, 0, g] = first
            PS[s, 1, g] = last

        each(0, nchunk, pack)
        groups = HALF // REACH
        done = []
        for dy, side, buf in ((1, 1, YPB), (-1, 0, YPC)):
            done.append(
                Copy(PS.at[s, side], buf.at[s, groups : groups + nchunk], (0, dy, 0))
            )
            done.append(
                Copy(
                    PS.at[s, side, 0:groups],
                    buf.at[s, groups + nchunk : 2 * groups + nchunk],
                    (-1, dy, 0),
                )
            )
            done.append(
                Copy(
                    PS.at[s, side, nchunk - groups : nchunk],
                    buf.at[s, 0:groups],
                    (1, dy, 0),
                )
            )
        return done

    order = [0] + [nchunk - 1] * (nchunk > 1) + list(range(1, nchunk - 1))
    xw, yw, zw = {}, {}, {}
    xw[1] = send_x(1, 0, REACH)
    for c in order:
        yw[1, c] = send_y(1, c)
        zw[1, c] = send_z(1, c * REACH, (c + 1) * REACH)

    x_start, y_start, z_start = ix * tx, iy * ty, iz * tz

    def load_rest(x):
        F[0, H + x] = weave(1, x, sp[x], rp[x])
        damping = ab[x].astype(jnp.float32) / 16.0
        inverse = 1.0 / (1.0 + damping)
        c2 = cr[x] * inverse
        a2 = 2.0 * inverse + (3.0 * centre_weight) * c2
        b2 = (damping - 1.0) * inverse
        CA[x] = weave(2, x, a2, a2)
        CB[x] = weave(3, x, b2, b2)
        CC[x] = weave(4, x, c2, c2)
        rows = x * 8 + lax.broadcasted_iota(jnp.int32, (8, rc.shape[1]), 0)
        y_of = rc[1:2, :] - y_start
        where = (rc[0:1, :] - x_start) * 8 + y_of * 2 + 1
        where = jnp.where((y_of >= 0) & (y_of < ty), where, -1)
        top = jnp.where(iz == 0, 1.0, 0.0)
        for t in range(STEPS):
            total = jnp.sum(
                jnp.where(rows == where, tr[t : t + 1, :], 0.0), axis=1, keepdims=True
            )
            INJ[t, x] = jnp.where(lane == 0, total * top, 0.0)

    each(0, tx, load_rest)
    point = jnp.where(
        (lane_z == cell[2] - z_start) & (sub_z == (cell[1] - y_start) * 2), 1.0, 0.0
    )
    source_x = cell[0] - x_start

    def merge(f, s, low, high):
        def body(x):
            E[s, x] = jnp.where(lane < LANES // 2, ZR[f - 1, x], ZL[f - 1, x])

        each(H + low, H + high, body)

    def advance(t, c):
        f = t + 1

        def body(j):
            x = c * REACH + j
            cur = F[f, H + x]
            below, above = YB[t, x], YC[t, x]
            edge = jnp.where(lane < LANES // 2, ZR[t, H + x], ZL[t, H + x])
            row = jnp.concatenate([cur, edge], axis=1)
            wide = tz + LANES
            total = None
            for k, w in ((1, W1), (2, W2), (3, W3), (4, W4)):
                part = F[f, H + x + k] + F[f, H + x - k]
                part = part + (pltpu.roll(row, k, 1) + pltpu.roll(row, wide - k, 1))[:, :tz]
                if k == 4:
                    part = part + (above + below)
                total = w * part if total is None else total + w * part

            def up(k):
                return jnp.where(sub_z < 2 * k, above, cur)

            def down(k):
                return jnp.where(sub_z >= 8 - 2 * k, below, cur)

            total = total + pltpu.roll(W1 * up(1) + W3 * down(3), 6, 0)
            total = total + pltpu.roll(W2 * (up(2) + down(2)), 4, 0)
            total = total + pltpu.roll(W3 * up(3) + W1 * down(1), 2, 0)
            new = CA[x] * cur + CB[x] * F[f - 1, H + x] + CC[x] * total
            new = new + point * (wav[t] * (source_x == x).astype(jnp.float32))
            F[f + 1, H + x] = new
            F[f + 1, H + x, :, 0:LANES] = new[:, 0:LANES] + INJ[t, x]

        each(0, REACH, body, unroll=2)

    late = {}
    snaps = [t + 2 for t in range(STEPS) if (t + 1) % EVERY == 0]
    for t in range(STEPS):
        f = t + 1
        nf = f + 1
        last = t == STEPS - 1
        for number, c in enumerate(order):
            if number == 0:
                xw[f][1].wait()
                if nchunk == 1:
                    xw[f][0].wait()
            if number == 1:
                xw[f][0].wait()
            for w in yw[f, c] + zw[f, c]:
                w.wait()
            advance(t, c)
            if not last:
                yw[nf, c] = send_y(nf, c)
                zw[nf, c] = send_z(nf, c * REACH, (c + 1) * REACH)
                if number == min(1, nchunk - 1):
                    xw[nf] = send_x(nf, 0, REACH)
        if nf in snaps:
            s = snaps.index(nf)
            late[s] = list(send_x(nf, 0 if last else REACH, H))
            if last:
                late[s] += send_z(nf, 0, tx)
            late[s] += send_rows(nf, s)
            late[s] += send_z(nf, 0, HALF, -1)
            late[s] += send_z(nf, tx - HALF, tx, 1)

    def out_fields(x):
        out_s[x], out_r[x] = unweave(x, F[STEPS + 1, H + x], (even, odd))

    each(0, tx, out_fields)

    def swap(v):
        parity = lax.broadcasted_iota(jnp.int32, v.shape, 0) % 2
        return jnp.where(parity == 0, pltpu.roll(v, 7, 0), pltpu.roll(v, 1, 0))

    for s, f in enumerate(snaps):
        for w in late[s]:
            w.wait()
        merge(f, s, -HALF, tx + HALF)

        def swapped(x, s=s, f=f):
            G[s, x] = swap(F[f, x])

        each(0, tx + 2 * H, swapped)

        def swapped_edge(x, s=s):
            GE[s, x] = swap(E[s, x])

        each(H - HALF, H + tx + HALF, swapped_edge)

        def unpack(g, s=s):
            above, below = YPC[s, g], YPB[s, g]
            for j in range(REACH):
                first = pltpu.roll(above, (8 - 2 * j) % 8, 0) if j else above
                shift = (6 - 2 * j) % 8
                other = pltpu.roll(below, shift, 0) if shift else below
                both = jnp.where(sub_z < 4, first, other)
                D[s, g * REACH + j] = both
                DG[s, g * REACH + j] = swap(both)

        each(0, (tx + 2 * HALF) // REACH, unpack)

    nsnap = len(snaps)

    def image(m, keep_even, keep_odd):
        def product(x):
            a, b = HALF + x - m, HALF + x + m
            total = F[snaps[0], a] * G[0, b]
            for s in range(1, nsnap):
                total = total + F[snaps[s], a] * G[s, b]
            IM[x, :, 0:tz] = total

        each(0, tx + 2, product, unroll=2)

        def halo(x):
            a, b = H + x - m, H + x + m
            total = E[0, a] * GE[0, b]
            for s in range(1, nsnap):
                total = total + E[s, a] * GE[s, b]
            IM[x + 1, :, tz : tz + LANES] = total
            a, b = HALF + x - m, HALF + x + m
            total = D[0, a] * DG[0, b]
            for s in range(1, nsnap):
                total = total + D[s, a] * DG[s, b]
            IH[x] = total

        each(0, tx, halo, unroll=2)

        def laplace(x):
            row = IM[x + 1]
            centre, side = row[:, :tz], IH[x]
            wide = tz + LANES
            near = (pltpu.roll(row, 1, 1) + pltpu.roll(row, wide - 1, 1))[:, :tz]
            near = near + (IM[x, :, 0:tz] + IM[x + 2, :, 0:tz])
            near = near + pltpu.roll(jnp.where(sub_z < 2, side, centre), 6, 0)
            near = near + pltpu.roll(jnp.where(sub_z >= 6, side, centre), 2, 0)
            plus, minus = unweave(x, 6.0 * centre - near, (even, odd))
            if keep_even:
                out_i[HALF + m, x] = plus.astype(jnp.bfloat16)
            if keep_odd:
                out_i[HALF - m, x] = minus.astype(jnp.bfloat16)

        each(0, tx, laplace, unroll=2)

    image(0, True, False)
    each(1, HALF, lambda m: image(m, True, True))
    image(HALF, False, True)
    for c in copies:
        c.finish()


def local(
    source_prev,
    source_now,
    receiver_prev,
    receiver_now,
    courant,
    absorbing,
    source_cell,
    wavelet,
    receiver_cells,
    traces,
):
    tx, ty, tz = courant.shape
    nsnap = STEPS // EVERY
    nchunk = tx // REACH
    groups = (tx + 2 * HALF) // REACH
    f32 = jnp.float32
    vmem = pl.BlockSpec(memory_space=pltpu.VMEM)
    smem = pl.BlockSpec(memory_space=pltpu.SMEM)
    number = STEPS * (2 + 4 * nchunk) + nsnap * 14
    V = pltpu.VMEM
    return pl.pallas_call(
        kernel,
        out_shape=(
            jax.ShapeDtypeStruct((tx, ty, tz), f32),
            jax.ShapeDtypeStruct((tx, ty, tz), f32),
            jax.ShapeDtypeStruct((LAGS, tx, ty, tz), jnp.bfloat16),
        ),
        in_specs=[vmem] * 6 + [smem] * 2 + [vmem] * 2,
        out_specs=(vmem, vmem, vmem),
        scratch_shapes=[
            V((STEPS + 2, tx + 2 * H, 8, tz), f32),
            V((STEPS, tx, 8, tz), f32),
            V((STEPS, tx, 8, tz), f32),
            V((STEPS + 1, tx + 2 * H, 8, LANES), f32),
            V((STEPS + 1, tx + 2 * H, 8, LANES), f32),
            V((nsnap, 2, nchunk, 8, tz), f32),
            V((nsnap, groups, 8, tz), f32),
            V((nsnap, groups, 8, tz), f32),
            V((nsnap, tx + 2 * H, 8, LANES), f32),
            V((nsnap, tx + 2 * H, 8, tz), f32),
            V((nsnap, tx + 2 * H, 8, LANES), f32),
            V((nsnap, tx + 2 * HALF, 8, tz), f32),
            V((nsnap, tx + 2 * HALF, 8, tz), f32),
            V((tx, 8, tz), f32),
            V((tx, 8, tz), f32),
            V((tx, 8, tz), f32),
            V((STEPS, tx, 8, LANES), f32),
            V((tx + 2, 8, tz + LANES), f32),
            V((tx, 8, tz), f32),
            V((tx, tz // LANES, 8, LANES), f32),
            V((5, tx, tz // LANES, 8, LANES), f32),
            pltpu.SemaphoreType.DMA((number,)),
            pltpu.SemaphoreType.DMA((number,)),
        ],
        compiler_params=pltpu.CompilerParams(
            collective_id=0, has_side_effects=True, vmem_limit_bytes=40 * 2**20
        ),
    )(
        source_prev,
        source_now,
        receiver_prev,
        receiver_now,
        courant,
        absorbing,
        source_cell,
        wavelet,
        receiver_cells.T,
        traces,
    )


def solution(mesh):
    placed = (
        P(("shot", "gx"), "gy", "gz"),
        P(("shot", "gx"), "gy", "gz"),
        P(("shot", "gx"), "gy", "gz"),
        P(("shot", "gx"), "gy", "gz"),
        P("gx", "gy", "gz"),
        P("gx", "gy", "gz"),
        P("shot"),
        P("shot"),
        P("shot", None),
        P(None, "shot"),
    )
    return jax.shard_map(
        local,
        mesh=mesh,
        in_specs=placed,
        out_specs=(
            P(("shot", "gx"), "gy", "gz"),
            P(("shot", "gx"), "gy", "gz"),
            P(None, ("shot", "gx"), "gy", "gz"),
        ),
        check_vma=False,
    )
```

time: 201 us -> 51.6 us (0.26)
  starting transfers between devices: 82.8 us -> 0 us
  waiting for transfers between devices: 55.4 us -> 0 us
  Pallas kernels: 0 us -> 41.1 us
  other arithmetic: 28.3 us -> 0 us
  local copies, waits for them, and re-layouts: 29.4 us -> 9.52 us
    ppermute x34 -> x0, starting transfers between devices: 82.8 us -> none  [the longest x17 60.7 us: with_halo(): before = lax.ppermute(last, axis, up)]
    ppermute x34 -> x0, waiting for transfers between devices: 55.4 us -> none  [the longest x17 28.4 us: with_halo(): after = lax.ppermute(first, axis, down)]
    pallas_call x0 -> x1, Pallas kernels: none -> 41.1 us  [local(): pl.pallas_call(kernel, out_shape=(jax.ShapeDtypeStruct((tx, ty, tz), f32)...]
    slice x5 -> x0, other arithmetic: 8.39 us -> none  [the longest x4 8.14 us: window(): padded[..., start_x:start_x + size_x, start_y:start_y + size_y, start_z:s...]
    another operation x6 -> x0, local copies, waits for them, and re-layouts: 7.31 us -> none  [the longest x2 6.85 us: correlate(): jnp.stack([widened[0, LAGS - offset:LAGS - offset + length] * widened[1,...]
    slice x16 -> x0, local copies, waits for them, and re-layouts: 7.09 us -> none  [the longest x8 3.47 us: with_halo(): first = lax.slice_in_dim(array, 0, width, axis=dim)]
    convert_element_type x4 -> x0, other arithmetic: 5.25 us -> none  [the longest x1 3.33 us: local(): filtered_image = laplace(framed).astype(jnp.bfloat16)]
    div x4 -> x0, other arithmetic: 4.61 us -> none  [advance(): (2.0 * current - (1.0 - damping) * earlier + courant * stencil(padded)) /...]
  transfers between devices with their start and end apart: 34 -> 0, of which waited for: 23 -> 0; matrix products, arithmetic and copies ran while one was open for 9% -> 0% of each run, Pallas kernels for 0% -> 0%
where the time goes in v1:
time: 51.6 us; the launch traced here: 51.3 us
  Pallas kernels  41.1 us (80%)
  local copies, waits for them, and re-layouts  9.52 us (18%)
  between operations  0.67 us (1%)
    pallas_call x1, Pallas kernels, local(): pl.pallas_call(kernel, out_shape=(jax.ShapeDtypeStruct((tx, ty, tz), f32)...  41.1 us
    unnamed x23, local copies, waits for them, and re-layouts  9.52 us

profile of v1, /device:TPU:0, one launch (start us, length us, event | category | flops | bytes accessed | tf_op | source)
XLA Modules:
  0.0 51.3 jit_solution(8294769660109435243)
XLA Ops:
  0.6 0.0 copy-start.7
  0.6 0.0 copy-start.8
  0.7 0.7 %copy-done.7 = s32[128,2]{0,1:T(2,128)S(1)} copy-done((s32[128,2]{0,1:T(2,128)S(1)}, s32[128,2]{0,1:T(2,128)}, u32[]{:S(2)}) %copy-start.7) | copy-done | bytes 1048
  1.3 0.0 copy-done.8
  1.3 0.0 copy-start
  1.3 0.9 %copy-done = f32[12,4,512]{2,1,0:T(4,128)S(1)} copy-done((f32[12,4,512]{2,1,0:T(4,128)S(1)}, f32[12,4,512]{2,1,0:T(4,128)}, u32[]{:S(2)}) %copy-start) | copy-done | bytes 98328
  2.2 0.0 copy-start.1
  2.2 0.9 %copy-done.1 = f32[12,4,512]{2,1,0:T(4,128)S(1)} copy-done((f32[12,4,512]{2,1,0:T(4,128)S(1)}, f32[12,4,512]{2,1,0:T(4,128)}, u32[]{:S(2)}) %copy-start.1) | copy-done | bytes 98328
  3.1 0.0 copy-start.2
  3.1 0.9 %copy-done.2 = f32[12,4,512]{2,1,0:T(4,128)S(1)} copy-done((f32[12,4,512]{2,1,0:T(4,128)S(1)}, f32[12,4,512]{2,1,0:T(4,128)}, u32[]{:S(2)}) %copy-start.2) | copy-done | bytes 98328
  4.0 0.0 copy-start.3
  4.0 0.9 %copy-done.3 = f32[12,4,512]{2,1,0:T(4,128)S(1)} copy-done((f32[12,4,512]{2,1,0:T(4,128)S(1)}, f32[12,4,512]{2,1,0:T(4,128)}, u32[]{:S(2)}) %copy-start.3) | copy-done | bytes 98328
  4.9 0.0 copy-start.4
  4.9 0.9 %copy-done.4 = f32[12,4,512]{2,1,0:T(4,128)S(1)} copy-done((f32[12,4,512]{2,1,0:T(4,128)S(1)}, f32[12,4,512]{2,1,0:T(4,128)}, u32[]{:S(2)}) %copy-start.4) | copy-done | bytes 98328
  5.8 0.0 copy-start.5
  5.8 0.9 %copy-done.5 = s32[12,4,512]{2,1,0:T(4,128)S(1)} copy-done((s32[12,4,512]{2,1,0:T(4,128)S(1)}, s32[12,4,512]{2,1,0:T(4,128)}, u32[]{:S(2)}) %copy-start.5) | copy-done | bytes 98328
  6.7 0.0 copy-start.6
  6.7 0.7 %copy-done.6 = f32[4,128]{1,0:T(4,128)S(1)} copy-done((f32[4,128]{1,0:T(4,128)S(1)}, f32[4,128]{1,0:T(4,128)}, u32[]{:S(2)}) %copy-start.6) | copy-done | bytes 2072
  7.4 0.0 copy-start.9
  7.4 0.7 %copy-done.9 = f32[4]{0:T(128)S(1)} copy-done((f32[4]{0:T(128)S(1)}, f32[4]{0:T(128)}, u32[]{:S(2)}) %copy-start.9) | copy-done | bytes 40
  8.0 41.1 %shard_map.121 = (f32[12,4,512]{2,1,0:T(4,128)S(1)}, f32[12,4,512]{2,1,0:T(4,128)S(1)}, bf16[16,12,4,512]{3,2,1,0:T(4,128)(2,1)S(1)}) custom-call(f32[12,4,512]{2,1,0:T(4,128)S(1)} %copy-done, f32[12,4,512]{2,1,0:T(4,128)S(1)} %copy-done.1, f32[12,4,512]{2,1,0:T(4,128)S(1)} %copy-done.2, f32[12,4,512]{2,1,0:T(4,128)S(1)} %copy-done.3, ...), custom_call_target="tpu_custom_call" | custom-call | tf_op jit(solution)/shard_map/pallas_call | solution.py:426
  49.1 0.6 %copy.16 = f32[12,4,512]{2,1,0:T(4,128)} copy(f32[12,4,512]{2,1,0:T(4,128)S(1)} %get-tuple-element.6) | data formatting | bytes 196608
  49.7 0.6 %copy.17 = f32[12,4,512]{2,1,0:T(4,128)} copy(f32[12,4,512]{2,1,0:T(4,128)S(1)} %get-tuple-element.7) | data formatting | bytes 196608
  50.4 0.9 %copy.18 = bf16[16,12,4,512]{3,2,1,0:T(4,128)(2,1)} copy(bf16[16,12,4,512]{3,2,1,0:T(4,128)(2,1)S(1)} %get-tuple-element.8) | data formatting | bytes 1572864
Async XLA Ops:
  0.6 0.7 %copy-start.7 = (s32[128,2]{0,1:T(2,128)S(1)}, s32[128,2]{0,1:T(2,128)}, u32[]{:S(2)}) copy-start(s32[128,2]{0,1:T(2,128)} %param.18) | copy-start | bytes 3076
  0.6 0.7 %copy-start.8 = (s32[3]{0:T(128)S(1)}, s32[3]{0:T(128)}, u32[]{:S(2)}) copy-start(s32[3]{0:T(128)} %cell.1) | copy-start | bytes 40
  1.3 0.9 %copy-start = (f32[12,4,512]{2,1,0:T(4,128)S(1)}, f32[12,4,512]{2,1,0:T(4,128)}, u32[]{:S(2)}) copy-start(f32[12,4,512]{2,1,0:T(4,128)} %sp.1) | copy-start | bytes 294916
  2.2 0.9 %copy-start.1 = (f32[12,4,512]{2,1,0:T(4,128)S(1)}, f32[12,4,512]{2,1,0:T(4,128)}, u32[]{:S(2)}) copy-start(f32[12,4,512]{2,1,0:T(4,128)} %sn.1) | copy-start | bytes 294916
  3.1 0.9 %copy-start.2 = (f32[12,4,512]{2,1,0:T(4,128)S(1)}, f32[12,4,512]{2,1,0:T(4,128)}, u32[]{:S(2)}) copy-start(f32[12,4,512]{2,1,0:T(4,128)} %rp.1) | copy-start | bytes 294916
  4.0 0.9 %copy-start.3 = (f32[12,4,512]{2,1,0:T(4,128)S(1)}, f32[12,4,512]{2,1,0:T(4,128)}, u32[]{:S(2)}) copy-start(f32[12,4,512]{2,1,0:T(4,128)} %rn.1) | copy-start | bytes 294916
  4.9 0.9 %copy-start.4 = (f32[12,4,512]{2,1,0:T(4,128)S(1)}, f32[12,4,512]{2,1,0:T(4,128)}, u32[]{:S(2)}) copy-start(f32[12,4,512]{2,1,0:T(4,128)} %cr.1) | copy-start | bytes 294916
  5.8 0.9 %copy-start.5 = (s32[12,4,512]{2,1,0:T(4,128)S(1)}, s32[12,4,512]{2,1,0:T(4,128)}, u32[]{:S(2)}) copy-start(s32[12,4,512]{2,1,0:T(4,128)} %ab.1) | copy-start | bytes 294916
  6.7 0.7 %copy-start.6 = (f32[4,128]{1,0:T(4,128)S(1)}, f32[4,128]{1,0:T(4,128)}, u32[]{:S(2)}) copy-start(f32[4,128]{1,0:T(4,128)} %tr.1) | copy-start | bytes 6148
  7.4 0.7 %copy-start.9 = (f32[4]{0:T(128)S(1)}, f32[4]{0:T(128)}, u32[]{:S(2)}) copy-start(f32[4]{0:T(128)} %wav.1) | copy-start | bytes 52

commit v2 on v1

--- a/solution.py
+++ b/solution.py
@@ -20,11 +20,23 @@
 
 
 def kernel(
+    sp_in, sn_in, rp_in, rn_in, cr_in, ab_in, cell_in, wav_in, rc_in, tr_in,
+    out_s, out_r, out_i,
+    F, YB, YC, ZL, ZR, PS, YPB, YPC, E, G, GE, D, DG, CA, CB, CC, INJ, LP, ST,
     sp, sn, rp, rn, cr, ab, cell, wav, rc, tr,
-    out_s, out_r, out_i,
-    F, YB, YC, ZL, ZR, PS, YPB, YPC, E, G, GE, D, DG, CA, CB, CC, INJ, IM, IH, LP, ST,
-    send, recv,
+    send, recv, fetch,
 ):
+    fetched = [
+        pltpu.make_async_copy(src, dst, fetch.at[i])
+        for i, (src, dst) in enumerate(
+            (
+                (sn_in, sn), (rn_in, rn), (sp_in, sp), (rp_in, rp), (cr_in, cr),
+                (ab_in, ab), (cell_in, cell), (wav_in, wav), (rc_in, rc), (tr_in, tr),
+            )
+        )
+    ]
+    for c in fetched:
+        c.start()
     tx, ty, tz = sn.shape
     nchunk = tx // REACH
     nx, ny, nz = (lax.axis_size(a) for a in ("gx", "gy", "gz"))
@@ -97,8 +109,6 @@
     def load_now(x):
         F[1, H + x] = weave(0, x, sn[x], rn[x])
 
-    each(0, tx, load_now)
-
     low_x, high_x = ix == 0, ix == nx - 1
     low_y, high_y = iy == 0, iy == ny - 1
     low_z, high_z = iz == 0, iz == nz - 1
@@ -144,6 +154,9 @@
                 barrier, inc=1, device_id=device(*direction), device_id_type=MESH
             )
 
+    for c in fetched[:2]:
+        c.wait()
+    each(0, tx, load_now, unroll=4)
     pl.semaphore_wait(barrier, count)
 
     def send_x(f, low, high):
@@ -241,17 +254,45 @@
             )
             INJ[t, x] = jnp.where(lane == 0, total * top, 0.0)
 
-    each(0, tx, load_rest)
+    for c in fetched[2:]:
+        c.wait()
+    each(0, tx, load_rest, unroll=2)
     point = jnp.where(
         (lane_z == cell[2] - z_start) & (sub_z == (cell[1] - y_start) * 2), 1.0, 0.0
     )
     source_x = cell[0] - x_start
 
-    def merge(f, s, low, high):
-        def body(x):
-            E[s, x] = jnp.where(lane < LANES // 2, ZR[f - 1, x], ZL[f - 1, x])
-
-        each(H + low, H + high, body)
+    def swap(v):
+        parity = lax.broadcasted_iota(jnp.int32, v.shape, 0) % 2
+        return jnp.where(parity == 0, pltpu.roll(v, 7, 0), pltpu.roll(v, 1, 0))
+
+    def prepare(s, f):
+        for w in late[s]:
+            w.wait()
+
+        def swapped(x):
+            G[s, x] = swap(F[f, x])
+
+        each(0, tx + 2 * H, swapped, unroll=5)
+
+        def edges(x):
+            edge = jnp.where(lane < LANES // 2, ZR[f - 1, x], ZL[f - 1, x])
+            E[s, x] = edge
+            GE[s, x] = swap(edge)
+
+        each(H - HALF, H + tx + HALF, edges, unroll=4)
+
+        def unpack(g):
+            above, below = YPC[s, g], YPB[s, g]
+            for j in range(REACH):
+                first = pltpu.roll(above, (8 - 2 * j) % 8, 0) if j else above
+                shift = (6 - 2 * j) % 8
+                other = pltpu.roll(below, shift, 0) if shift else below
+                both = jnp.where(sub_z < 4, first, other)
+                D[s, g * REACH + j] = both
+                DG[s, g * REACH + j] = swap(both)
+
+        each(0, (tx + 2 * HALF) // REACH, unpack)
 
     def advance(t, c):
         f = t + 1
@@ -316,44 +357,17 @@
             late[s] += send_rows(nf, s)
             late[s] += send_z(nf, 0, HALF, -1)
             late[s] += send_z(nf, tx - HALF, tx, 1)
+        elif snaps[0] < nf:
+            prepare(0, snaps[0])
 
     def out_fields(x):
         out_s[x], out_r[x] = unweave(x, F[STEPS + 1, H + x], (even, odd))
 
-    each(0, tx, out_fields)
-
-    def swap(v):
-        parity = lax.broadcasted_iota(jnp.int32, v.shape, 0) % 2
-        return jnp.where(parity == 0, pltpu.roll(v, 7, 0), pltpu.roll(v, 1, 0))
-
-    for s, f in enumerate(snaps):
-        for w in late[s]:
-            w.wait()
-        merge(f, s, -HALF, tx + HALF)
-
-        def swapped(x, s=s, f=f):
-            G[s, x] = swap(F[f, x])
-
-        each(0, tx + 2 * H, swapped)
-
-        def swapped_edge(x, s=s):
-            GE[s, x] = swap(E[s, x])
-
-        each(H - HALF, H + tx + HALF, swapped_edge)
-
-        def unpack(g, s=s):
-            above, below = YPC[s, g], YPB[s, g]
-            for j in range(REACH):
-                first = pltpu.roll(above, (8 - 2 * j) % 8, 0) if j else above
-                shift = (6 - 2 * j) % 8
-                other = pltpu.roll(below, shift, 0) if shift else below
-                both = jnp.where(sub_z < 4, first, other)
-                D[s, g * REACH + j] = both
-                DG[s, g * REACH + j] = swap(both)
-
-        each(0, (tx + 2 * HALF) // REACH, unpack)
+    each(0, tx, out_fields, unroll=4)
 
     nsnap = len(snaps)
+    for s in range(1, nsnap):
+        prepare(s, snaps[s])
 
     def image(m, keep_even, keep_odd):
         def product(x):
@@ -361,30 +375,27 @@
             total = F[snaps[0], a] * G[0, b]
             for s in range(1, nsnap):
                 total = total + F[snaps[s], a] * G[s, b]
-            IM[x, :, 0:tz] = total
-
-        each(0, tx + 2, product, unroll=2)
+            return total
 
         def halo(x):
             a, b = H + x - m, H + x + m
-            total = E[0, a] * GE[0, b]
+            edge = E[0, a] * GE[0, b]
             for s in range(1, nsnap):
-                total = total + E[s, a] * GE[s, b]
-            IM[x + 1, :, tz : tz + LANES] = total
+                edge = edge + E[s, a] * GE[s, b]
             a, b = HALF + x - m, HALF + x + m
-            total = D[0, a] * DG[0, b]
+            side = D[0, a] * DG[0, b]
             for s in range(1, nsnap):
-                total = total + D[s, a] * DG[s, b]
-            IH[x] = total
-
-        each(0, tx, halo, unroll=2)
-
-        def laplace(x):
-            row = IM[x + 1]
-            centre, side = row[:, :tz], IH[x]
+                side = side + D[s, a] * DG[s, b]
+            return edge, side
+
+        before, centre = product(0), product(1)
+        for x in range(tx):
+            after = product(x + 2)
+            edge, side = halo(x)
+            row = jnp.concatenate([centre, edge], axis=1)
             wide = tz + LANES
             near = (pltpu.roll(row, 1, 1) + pltpu.roll(row, wide - 1, 1))[:, :tz]
-            near = near + (IM[x, :, 0:tz] + IM[x + 2, :, 0:tz])
+            near = near + (before + after)
             near = near + pltpu.roll(jnp.where(sub_z < 2, side, centre), 6, 0)
             near = near + pltpu.roll(jnp.where(sub_z >= 6, side, centre), 2, 0)
             plus, minus = unweave(x, 6.0 * centre - near, (even, odd))
@@ -392,8 +403,7 @@
                 out_i[HALF + m, x] = plus.astype(jnp.bfloat16)
             if keep_odd:
                 out_i[HALF - m, x] = minus.astype(jnp.bfloat16)
-
-        each(0, tx, laplace, unroll=2)
+            before, centre = centre, after
 
     image(0, True, False)
     each(1, HALF, lambda m: image(m, True, True))
@@ -420,7 +430,6 @@
     groups = (tx + 2 * HALF) // REACH
     f32 = jnp.float32
     vmem = pl.BlockSpec(memory_space=pltpu.VMEM)
-    smem = pl.BlockSpec(memory_space=pltpu.SMEM)
     number = STEPS * (2 + 4 * nchunk) + nsnap * 14
     V = pltpu.VMEM
     return pl.pallas_call(
@@ -430,7 +439,7 @@
             jax.ShapeDtypeStruct((tx, ty, tz), f32),
             jax.ShapeDtypeStruct((LAGS, tx, ty, tz), jnp.bfloat16),
         ),
-        in_specs=[vmem] * 6 + [smem] * 2 + [vmem] * 2,
+        in_specs=[pl.BlockSpec(memory_space=pltpu.HBM)] * 10,
         out_specs=(vmem, vmem, vmem),
         scratch_shapes=[
             V((STEPS + 2, tx + 2 * H, 8, tz), f32),
@@ -450,12 +459,17 @@
             V((tx, 8, tz), f32),
             V((tx, 8, tz), f32),
             V((STEPS, tx, 8, LANES), f32),
-            V((tx + 2, 8, tz + LANES), f32),
-            V((tx, 8, tz), f32),
             V((tx, tz // LANES, 8, LANES), f32),
             V((5, tx, tz // LANES, 8, LANES), f32),
+            *[V((tx, ty, tz), f32) for _ in range(5)],
+            V((tx, ty, tz), jnp.int32),
+            pltpu.SMEM(source_cell.shape, jnp.int32),
+            pltpu.SMEM(wavelet.shape, f32),
+            V(receiver_cells.shape[::-1], jnp.int32),
+            V(traces.shape, f32),
             pltpu.SemaphoreType.DMA((number,)),
             pltpu.SemaphoreType.DMA((number,)),
+            pltpu.SemaphoreType.DMA((10,)),
         ],
         compiler_params=pltpu.CompilerParams(
             collective_id=0, has_side_effects=True, vmem_limit_bytes=40 * 2**20

time: 51.6 us -> 46.4 us (0.90)
  Pallas kernels: 41.1 us -> 35.8 us
    pallas_call x1, Pallas kernels: 41.1 us -> 35.8 us  [local(): pl.pallas_call(kernel, out_shape=(jax.ShapeDtypeStruct((tx, ty, tz), f32)...]
where the time goes in v2:
time: 46.4 us; the launch traced here: 46 us
  Pallas kernels  35.8 us (77%)
  local copies, waits for them, and re-layouts  9.52 us (21%)
  between operations  0.67 us (1%)
    pallas_call x1, Pallas kernels, local(): pl.pallas_call(kernel, out_shape=(jax.ShapeDtypeStruct((tx, ty, tz), f32)...  35.8 us
    unnamed x23, local copies, waits for them, and re-layouts  9.52 us

profile of v2, /device:TPU:0, one launch (start us, length us, event | category | flops | bytes accessed | tf_op | source)
XLA Modules:
  0.0 46.0 jit_solution(4240281250656494751)
XLA Ops:
  0.6 0.0 copy-start.7
  0.6 0.0 copy-start.8
  0.7 0.7 %copy-done.7 = s32[128,2]{0,1:T(2,128)S(1)} copy-done((s32[128,2]{0,1:T(2,128)S(1)}, s32[128,2]{0,1:T(2,128)}, u32[]{:S(2)}) %copy-start.7) | copy-done | bytes 1048
  1.3 0.0 copy-done.8
  1.3 0.0 copy-start
  1.3 0.9 %copy-done = f32[12,4,512]{2,1,0:T(4,128)S(1)} copy-done((f32[12,4,512]{2,1,0:T(4,128)S(1)}, f32[12,4,512]{2,1,0:T(4,128)}, u32[]{:S(2)}) %copy-start) | copy-done | bytes 98328
  2.2 0.0 copy-start.1
  2.2 0.9 %copy-done.1 = f32[12,4,512]{2,1,0:T(4,128)S(1)} copy-done((f32[12,4,512]{2,1,0:T(4,128)S(1)}, f32[12,4,512]{2,1,0:T(4,128)}, u32[]{:S(2)}) %copy-start.1) | copy-done | bytes 98328
  3.1 0.0 copy-start.2
  3.1 0.9 %copy-done.2 = f32[12,4,512]{2,1,0:T(4,128)S(1)} copy-done((f32[12,4,512]{2,1,0:T(4,128)S(1)}, f32[12,4,512]{2,1,0:T(4,128)}, u32[]{:S(2)}) %copy-start.2) | copy-done | bytes 98328
  4.0 0.0 copy-start.3
  4.0 0.9 %copy-done.3 = f32[12,4,512]{2,1,0:T(4,128)S(1)} copy-done((f32[12,4,512]{2,1,0:T(4,128)S(1)}, f32[12,4,512]{2,1,0:T(4,128)}, u32[]{:S(2)}) %copy-start.3) | copy-done | bytes 98328
  4.9 0.0 copy-start.4
  4.9 0.9 %copy-done.4 = f32[12,4,512]{2,1,0:T(4,128)S(1)} copy-done((f32[12,4,512]{2,1,0:T(4,128)S(1)}, f32[12,4,512]{2,1,0:T(4,128)}, u32[]{:S(2)}) %copy-start.4) | copy-done | bytes 98328
  5.8 0.0 copy-start.5
  5.8 0.9 %copy-done.5 = s32[12,4,512]{2,1,0:T(4,128)S(1)} copy-done((s32[12,4,512]{2,1,0:T(4,128)S(1)}, s32[12,4,512]{2,1,0:T(4,128)}, u32[]{:S(2)}) %copy-start.5) | copy-done | bytes 98328
  6.7 0.0 copy-start.6
  6.7 0.7 %copy-done.6 = f32[4,128]{1,0:T(4,128)S(1)} copy-done((f32[4,128]{1,0:T(4,128)S(1)}, f32[4,128]{1,0:T(4,128)}, u32[]{:S(2)}) %copy-start.6) | copy-done | bytes 2072
  7.4 0.0 copy-start.9
  7.4 0.7 %copy-done.9 = f32[4]{0:T(128)S(1)} copy-done((f32[4]{0:T(128)S(1)}, f32[4]{0:T(128)}, u32[]{:S(2)}) %copy-start.9) | copy-done | bytes 40
  8.0 35.8 %shard_map.121 = (f32[12,4,512]{2,1,0:T(4,128)S(1)}, f32[12,4,512]{2,1,0:T(4,128)S(1)}, bf16[16,12,4,512]{3,2,1,0:T(4,128)(2,1)S(1)}) custom-call(f32[12,4,512]{2,1,0:T(4,128)S(1)} %copy-done, f32[12,4,512]{2,1,0:T(4,128)S(1)} %copy-done.1, f32[12,4,512]{2,1,0:T(4,128)S(1)} %copy-done.2, f32[12,4,512]{2,1,0:T(4,128)S(1)} %copy-done.3, ...), custom_call_target="tpu_custom_call" | custom-call | tf_op jit(solution)/shard_map/pallas_call | solution.py:435
  43.9 0.6 %copy.16 = f32[12,4,512]{2,1,0:T(4,128)} copy(f32[12,4,512]{2,1,0:T(4,128)S(1)} %get-tuple-element.6) | data formatting | bytes 196608
  44.5 0.6 %copy.17 = f32[12,4,512]{2,1,0:T(4,128)} copy(f32[12,4,512]{2,1,0:T(4,128)S(1)} %get-tuple-element.7) | data formatting | bytes 196608
  45.2 0.9 %copy.18 = bf16[16,12,4,512]{3,2,1,0:T(4,128)(2,1)} copy(bf16[16,12,4,512]{3,2,1,0:T(4,128)(2,1)S(1)} %get-tuple-element.8) | data formatting | bytes 1572864
Async XLA Ops:
  0.6 0.7 %copy-start.7 = (s32[128,2]{0,1:T(2,128)S(1)}, s32[128,2]{0,1:T(2,128)}, u32[]{:S(2)}) copy-start(s32[128,2]{0,1:T(2,128)} %param.18) | copy-start | bytes 3076
  0.6 0.7 %copy-start.8 = (s32[3]{0:T(128)S(1)}, s32[3]{0:T(128)}, u32[]{:S(2)}) copy-start(s32[3]{0:T(128)} %cell_in.1) | copy-start | bytes 40
  1.3 0.9 %copy-start = (f32[12,4,512]{2,1,0:T(4,128)S(1)}, f32[12,4,512]{2,1,0:T(4,128)}, u32[]{:S(2)}) copy-start(f32[12,4,512]{2,1,0:T(4,128)} %sp_in.1) | copy-start | bytes 294916
  2.2 0.9 %copy-start.1 = (f32[12,4,512]{2,1,0:T(4,128)S(1)}, f32[12,4,512]{2,1,0:T(4,128)}, u32[]{:S(2)}) copy-start(f32[12,4,512]{2,1,0:T(4,128)} %sn_in.1) | copy-start | bytes 294916
  3.1 0.9 %copy-start.2 = (f32[12,4,512]{2,1,0:T(4,128)S(1)}, f32[12,4,512]{2,1,0:T(4,128)}, u32[]{:S(2)}) copy-start(f32[12,4,512]{2,1,0:T(4,128)} %rp_in.1) | copy-start | bytes 294916
  4.0 0.9 %copy-start.3 = (f32[12,4,512]{2,1,0:T(4,128)S(1)}, f32[12,4,512]{2,1,0:T(4,128)}, u32[]{:S(2)}) copy-start(f32[12,4,512]{2,1,0:T(4,128)} %rn_in.1) | copy-start | bytes 294916
  4.9 0.9 %copy-start.4 = (f32[12,4,512]{2,1,0:T(4,128)S(1)}, f32[12,4,512]{2,1,0:T(4,128)}, u32[]{:S(2)}) copy-start(f32[12,4,512]{2,1,0:T(4,128)} %cr_in.1) | copy-start | bytes 294916
  5.8 0.9 %copy-start.5 = (s32[12,4,512]{2,1,0:T(4,128)S(1)}, s32[12,4,512]{2,1,0:T(4,128)}, u32[]{:S(2)}) copy-start(s32[12,4,512]{2,1,0:T(4,128)} %ab_in.1) | copy-start | bytes 294916
  6.7 0.7 %copy-start.6 = (f32[4,128]{1,0:T(4,128)S(1)}, f32[4,128]{1,0:T(4,128)}, u32[]{:S(2)}) copy-start(f32[4,128]{1,0:T(4,128)} %tr_in.1) | copy-start | bytes 6148
  7.4 0.7 %copy-start.9 = (f32[4]{0:T(128)S(1)}, f32[4]{0:T(128)}, u32[]{:S(2)}) copy-start(f32[4]{0:T(128)} %wav_in.1) | copy-start | bytes 52

commit v3 on v2

--- a/solution.py
+++ b/solution.py
@@ -188,40 +188,43 @@
             Copy(F.at[f, rows, :, pl.ds(0, LANES)], ZR.at[f - 1, there], (dx, 0, -1)),
         )
 
-    def send_rows(f, s):
-        def pack(g):
-            first, last = F[f, H + g * REACH], F[f, H + g * REACH]
-            last = pltpu.roll(last, 2, 0)
-            for j in range(1, REACH):
-                row = F[f, H + g * REACH + j]
-                here = sub_z // 2 == j
-                first = jnp.where(here, pltpu.roll(row, 2 * j, 0), first)
-                shift = (2 * j - 6) % 8
-                last = jnp.where(here, pltpu.roll(row, shift, 0) if shift else row, last)
-            PS[s, 0, g] = first
-            PS[s, 1, g] = last
-
-        each(0, nchunk, pack)
-        groups = HALF // REACH
+    groups = HALF // REACH
+
+    def gather(rows, first):
+        packed = None
+        for k in range(REACH):
+            row = rows[k]
+            shift = (2 * k - first) % 8
+            row = pltpu.roll(row, shift, 0) if shift else row
+            packed = row if packed is None else jnp.where(sub_z // 2 == k, row, packed)
+        return packed
+
+    def pass_on(src, buf, s, g, dy):
+        done = []
+        if g < groups:
+            done.append(Copy(src, buf.at[s, groups + nchunk + g], (-1, dy, 0)))
+        if g >= nchunk - groups:
+            done.append(Copy(src, buf.at[s, g - (nchunk - groups)], (1, dy, 0)))
+        return done
+
+    def send_rows(f, s, g):
+        rows = [F[f, H + g * REACH + k] for k in range(REACH)]
+        PS[s, 0, g] = gather(rows, 0)
+        PS[s, 1, g] = gather(rows, 6)
         done = []
         for dy, side, buf in ((1, 1, YPB), (-1, 0, YPC)):
-            done.append(
-                Copy(PS.at[s, side], buf.at[s, groups : groups + nchunk], (0, dy, 0))
+            src = PS.at[s, side, g]
+            done.append(Copy(src, buf.at[s, groups + g], (0, dy, 0)))
+            done += pass_on(src, buf, s, g, dy)
+        return done
+
+    def relay_rows(f, s, g):
+        done = []
+        for src, buf, first in ((YB, YPB, 6), (YC, YPC, 0)):
+            buf[s, groups + g] = gather(
+                [src[f - 1, g * REACH + k] for k in range(REACH)], first
             )
-            done.append(
-                Copy(
-                    PS.at[s, side, 0:groups],
-                    buf.at[s, groups + nchunk : 2 * groups + nchunk],
-                    (-1, dy, 0),
-                )
-            )
-            done.append(
-                Copy(
-                    PS.at[s, side, nchunk - groups : nchunk],
-                    buf.at[s, 0:groups],
-                    (1, dy, 0),
-                )
-            )
+            done += pass_on(buf.at[s, groups + g], buf, s, g, 0)
         return done
 
     order = [0] + [nchunk - 1] * (nchunk > 1) + list(range(1, nchunk - 1))
@@ -326,7 +329,7 @@
             F[f + 1, H + x] = new
             F[f + 1, H + x, :, 0:LANES] = new[:, 0:LANES] + INJ[t, x]
 
-        each(0, REACH, body, unroll=2)
+        each(0, REACH, body, unroll=REACH)
 
     late = {}
     snaps = [t + 2 for t in range(STEPS) if (t + 1) % EVERY == 0]
@@ -349,16 +352,21 @@
                 zw[nf, c] = send_z(nf, c * REACH, (c + 1) * REACH)
                 if number == min(1, nchunk - 1):
                     xw[nf] = send_x(nf, 0, REACH)
+            elif nf in snaps:
+                late.setdefault(snaps.index(nf), []).extend(send_rows(nf, snaps.index(nf), c))
+            if f in snaps:
+                late[snaps.index(f)] += relay_rows(f, snaps.index(f), c)
         if nf in snaps:
             s = snaps.index(nf)
-            late[s] = list(send_x(nf, 0 if last else REACH, H))
+            waits = late.setdefault(s, [])
+            waits += send_x(nf, 0 if last else REACH, H)
             if last:
-                late[s] += send_z(nf, 0, tx)
-            late[s] += send_rows(nf, s)
-            late[s] += send_z(nf, 0, HALF, -1)
-            late[s] += send_z(nf, tx - HALF, tx, 1)
-        elif snaps[0] < nf:
-            prepare(0, snaps[0])
+                waits += send_z(nf, 0, tx)
+            waits += send_z(nf, 0, HALF, -1)
+            waits += send_z(nf, tx - HALF, tx, 1)
+
+    for s, f in enumerate(snaps[:-1]):
+        prepare(s, f)
 
     def out_fields(x):
         out_s[x], out_r[x] = unweave(x, F[STEPS + 1, H + x], (even, odd))
@@ -366,8 +374,7 @@
     each(0, tx, out_fields, unroll=4)
 
     nsnap = len(snaps)
-    for s in range(1, nsnap):
-        prepare(s, snaps[s])
+    prepare(nsnap - 1, snaps[-1])
 
     def image(m, keep_even, keep_odd):
         def product(x):
@@ -430,7 +437,7 @@
     groups = (tx + 2 * HALF) // REACH
     f32 = jnp.float32
     vmem = pl.BlockSpec(memory_space=pltpu.VMEM)
-    number = STEPS * (2 + 4 * nchunk) + nsnap * 14
+    number = STEPS * (2 + 4 * nchunk) + nsnap * 20
     V = pltpu.VMEM
     return pl.pallas_call(
         kernel,
@@ -472,7 +479,7 @@
             pltpu.SemaphoreType.DMA((10,)),
         ],
         compiler_params=pltpu.CompilerParams(
-            collective_id=0, has_side_effects=True, vmem_limit_bytes=40 * 2**20
+            collective_id=0, has_side_effects=True, vmem_limit_bytes=63 * 2**20
         ),
     )(
         source_prev,

time: 46.4 us -> 39.4 us (0.85)
  local copies, waits for them, and re-layouts: 9.52 us -> 4.52 us
  Pallas kernels: 35.8 us -> 34 us
    unnamed x23 -> x5, local copies, waits for them, and re-layouts: 9.52 us -> 4.52 us
    pallas_call x1, Pallas kernels: 35.8 us -> 34 us  [local(): pl.pallas_call(kernel, out_shape=(jax.ShapeDtypeStruct((tx, ty, tz), f32)...]
where the time goes in v3:
time: 39.4 us; the launch traced here: 39.2 us
  Pallas kernels  34 us (86%)
  local copies, waits for them, and re-layouts  4.52 us (11%)
  between operations  0.65 us (2%)
    pallas_call x1, Pallas kernels, local(): pl.pallas_call(kernel, out_shape=(jax.ShapeDtypeStruct((tx, ty, tz), f32)...  34 us
    unnamed x5, local copies, waits for them, and re-layouts  4.52 us

profile of v3, /device:TPU:0, one launch (start us, length us, event | category | flops | bytes accessed | tf_op | source)
XLA Modules:
  0.0 39.2 jit_solution(5153329847086985720)
XLA Ops:
  0.6 34.0 %shard_map.121 = (f32[12,4,512]{2,1,0:T(4,128)}, f32[12,4,512]{2,1,0:T(4,128)}, bf16[16,12,4,512]{3,2,1,0:T(4,128)(2,1)}) custom-call(f32[12,4,512]{2,1,0:T(4,128)} %sp_in.1, f32[12,4,512]{2,1,0:T(4,128)} %sn_in.1, f32[12,4,512]{2,1,0:T(4,128)} %rp_in.1, f32[12,4,512]{2,1,0:T(4,128)} %rn_in.1, f32[12,4,512]{2,1,0:T(4,128)} %cr_in.1, s32[12,4,512]{2,1,0:T(4,128)} %ab_in.1, ...), custom_call_target="tpu_custom_call" | custom-call | tf_op jit(solution)/shard_map/pallas_call | solution.py:442
  34.6 0.0 copy-start
  34.6 1.6 %copy.16 = f32[12,4,512]{2,1,0:T(4,128)} copy(f32[12,4,512]{2,1,0:T(4,128)} %get-tuple-element.6) | data formatting | bytes 196608
  36.2 0.0 copy-done
  36.2 0.6 %copy.17 = f32[12,4,512]{2,1,0:T(4,128)} copy(f32[12,4,512]{2,1,0:T(4,128)S(1)} %copy-done) | data formatting | bytes 196608
  36.9 2.3 %copy.18 = bf16[16,12,4,512]{3,2,1,0:T(4,128)(2,1)} copy(bf16[16,12,4,512]{3,2,1,0:T(4,128)(2,1)} %get-tuple-element.8) | data formatting | bytes 1572864
Async XLA Ops:
  34.6 1.6 %copy-start = (f32[12,4,512]{2,1,0:T(4,128)S(1)}, f32[12,4,512]{2,1,0:T(4,128)}, u32[]{:S(2)}) copy-start(f32[12,4,512]{2,1,0:T(4,128)} %get-tuple-element.7) | copy-start | bytes 294916

commit v4 on v3

--- a/solution.py
+++ b/solution.py
@@ -21,24 +21,16 @@
 
 def kernel(
     sp_in, sn_in, rp_in, rn_in, cr_in, ab_in, cell_in, wav_in, rc_in, tr_in,
+    to_s, to_r, to_i,
     out_s, out_r, out_i,
     F, YB, YC, ZL, ZR, PS, YPB, YPC, E, G, GE, D, DG, CA, CB, CC, INJ, LP, ST,
     sp, sn, rp, rn, cr, ab, cell, wav, rc, tr,
-    send, recv, fetch,
+    send, recv, fetch, leave,
 ):
-    fetched = [
-        pltpu.make_async_copy(src, dst, fetch.at[i])
-        for i, (src, dst) in enumerate(
-            (
-                (sn_in, sn), (rn_in, rn), (sp_in, sp), (rp_in, rp), (cr_in, cr),
-                (ab_in, ab), (cell_in, cell), (wav_in, wav), (rc_in, rc), (tr_in, tr),
-            )
-        )
-    ]
-    for c in fetched:
-        c.start()
     tx, ty, tz = sn.shape
     nchunk = tx // REACH
+    snaps = [t + 2 for t in range(STEPS) if (t + 1) % EVERY == 0]
+    nsnap = len(snaps)
     nx, ny, nz = (lax.axis_size(a) for a in ("gx", "gy", "gz"))
     ix, iy, iz = (lax.axis_index(a) for a in ("gx", "gy", "gz"))
     copies = []
@@ -113,32 +105,6 @@
     low_y, high_y = iy == 0, iy == ny - 1
     low_z, high_z = iz == 0, iz == nz - 1
 
-    @pl.when(low_x)
-    def _():
-        for i in range(1, STEPS + 2):
-            F[i, 0:H] = jnp.zeros((H, 8, tz), jnp.float32)
-
-    @pl.when(high_x)
-    def _():
-        for i in range(1, STEPS + 2):
-            F[i, H + tx : 2 * H + tx] = jnp.zeros((H, 8, tz), jnp.float32)
-
-    for missing, buf, packed in ((low_y, YB, YPB), (high_y, YC, YPC)):
-
-        @pl.when(missing)
-        def _(buf=buf):
-            buf[...] = jnp.zeros(buf.shape, jnp.float32)
-
-        @pl.when(missing | low_x | high_x)
-        def _(packed=packed):
-            packed[...] = jnp.zeros(packed.shape, jnp.float32)
-
-    for missing, buf in ((low_z, ZL), (high_z, ZR)):
-
-        @pl.when(missing | low_x | high_x)
-        def _(buf=buf):
-            buf[...] = jnp.zeros(buf.shape, jnp.float32)
-
     signs = (-1, 1)
     around = [(s, 0, 0) for s in signs] + [(0, s, 0) for s in signs] + [(0, 0, s) for s in signs]
     around += [(s, r, 0) for s in signs for r in signs] + [(s, 0, r) for s in signs for r in signs]
@@ -154,6 +120,17 @@
                 barrier, inc=1, device_id=device(*direction), device_id_type=MESH
             )
 
+    fetched = [
+        pltpu.make_async_copy(src, dst, fetch.at[i])
+        for i, (src, dst) in enumerate(
+            (
+                (sn_in, sn), (rn_in, rn), (sp_in, sp), (rp_in, rp), (cr_in, cr),
+                (ab_in, ab), (cell_in, cell), (wav_in, wav), (rc_in, rc), (tr_in, tr),
+            )
+        )
+    ]
+    for c in fetched:
+        c.start()
     for c in fetched[:2]:
         c.wait()
     each(0, tx, load_now, unroll=4)
@@ -172,6 +149,20 @@
         )
         return left, right
 
+    def send_x_chunk(f, c):
+        done = []
+        low, high = c * REACH, min((c + 1) * REACH, H)
+        if low < high:
+            done.append(
+                Copy(F.at[f, H + low : H + high], F.at[f, H + tx + low : H + tx + high], (-1, 0, 0))
+            )
+        low, high = max(c * REACH, tx - H), (c + 1) * REACH
+        if low < high:
+            done.append(
+                Copy(F.at[f, H + low : H + high], F.at[f, H + low - tx : H + high - tx], (1, 0, 0))
+            )
+        return done
+
     def send_y(f, c):
         own = F.at[f, H + c * REACH : H + (c + 1) * REACH]
         there = pl.ds(c * REACH, REACH)
@@ -233,6 +224,25 @@
     for c in order:
         yw[1, c] = send_y(1, c)
         zw[1, c] = send_z(1, c * REACH, (c + 1) * REACH)
+
+    def zero(missing, *refs):
+        @pl.when(missing)
+        def _():
+            for ref in refs:
+                ref[...] = jnp.zeros(ref.shape, jnp.float32)
+
+    low_rows, high_rows = pl.ds(0, H), pl.ds(H + tx, H)
+    low_packs, high_packs = pl.ds(0, groups), pl.ds(groups + nchunk, groups)
+    zero(low_x, *[F.at[i, low_rows] for i in range(1, STEPS + 2)])
+    zero(high_x, *[F.at[i, high_rows] for i in range(1, STEPS + 2)])
+    zero(low_y, YB, YPB)
+    zero(high_y, YC, YPC)
+    zero(low_z, ZL)
+    zero(high_z, ZR)
+    zero(low_x, *[b.at[snaps[s] - 1, low_rows] for b in (ZL, ZR) for s in range(nsnap)])
+    zero(high_x, *[b.at[snaps[s] - 1, high_rows] for b in (ZL, ZR) for s in range(nsnap)])
+    zero(low_x, *[b.at[s, low_packs] for b in (YPB, YPC) for s in range(nsnap)])
+    zero(high_x, *[b.at[s, high_packs] for b in (YPB, YPC) for s in range(nsnap)])
 
     x_start, y_start, z_start = ix * tx, iy * ty, iz * tz
 
@@ -332,7 +342,6 @@
         each(0, REACH, body, unroll=REACH)
 
     late = {}
-    snaps = [t + 2 for t in range(STEPS) if (t + 1) % EVERY == 0]
     for t in range(STEPS):
         f = t + 1
         nf = f + 1
@@ -353,28 +362,37 @@
                 if number == min(1, nchunk - 1):
                     xw[nf] = send_x(nf, 0, REACH)
             elif nf in snaps:
-                late.setdefault(snaps.index(nf), []).extend(send_rows(nf, snaps.index(nf), c))
+                waits = late.setdefault(snaps.index(nf), [])
+                waits += send_x_chunk(nf, c)
+                waits += send_rows(nf, snaps.index(nf), c)
             if f in snaps:
                 late[snaps.index(f)] += relay_rows(f, snaps.index(f), c)
         if nf in snaps:
             s = snaps.index(nf)
             waits = late.setdefault(s, [])
-            waits += send_x(nf, 0 if last else REACH, H)
-            if last:
+            if not last:
+                waits += send_x(nf, REACH, H)
+            else:
                 waits += send_z(nf, 0, tx)
             waits += send_z(nf, 0, HALF, -1)
             waits += send_z(nf, tx - HALF, tx, 1)
 
-    for s, f in enumerate(snaps[:-1]):
-        prepare(s, f)
-
     def out_fields(x):
         out_s[x], out_r[x] = unweave(x, F[STEPS + 1, H + x], (even, odd))
 
     each(0, tx, out_fields, unroll=4)
-
-    nsnap = len(snaps)
-    prepare(nsnap - 1, snaps[-1])
+    leaving = [
+        pltpu.make_async_copy(out_s, to_s, leave.at[LAGS]),
+        pltpu.make_async_copy(out_r, to_r, leave.at[LAGS + 1]),
+    ]
+    for c in leaving:
+        c.start()
+
+    def lag_out(lag):
+        return pltpu.make_async_copy(out_i.at[lag], to_i.at[lag], leave.at[lag])
+
+    for s, f in enumerate(snaps):
+        prepare(s, f)
 
     def image(m, keep_even, keep_odd):
         def product(x):
@@ -411,12 +429,32 @@
             if keep_odd:
                 out_i[HALF - m, x] = minus.astype(jnp.bfloat16)
             before, centre = centre, after
+        if keep_even:
+            lag_out(HALF + m).start()
+        if keep_odd:
+            lag_out(HALF - m).start()
 
     image(0, True, False)
     each(1, HALF, lambda m: image(m, True, True))
     image(HALF, False, True)
     for c in copies:
         c.finish()
+    for c in leaving:
+        c.wait()
+    each(0, LAGS, lambda lag: lag_out(lag).wait())
+
+
+def deliver(s, r, i, out_s, out_r, out_i, sems):
+    pairs = [(s, out_s), (r, out_r)]
+    part = LAGS // 4
+    pairs += [
+        (i.at[k * part : (k + 1) * part], out_i.at[k * part : (k + 1) * part]) for k in range(4)
+    ]
+    moves = [pltpu.make_async_copy(a, b, sems.at[n]) for n, (a, b) in enumerate(pairs)]
+    for c in moves:
+        c.start()
+    for c in moves:
+        c.wait()
 
 
 def local(
@@ -436,19 +474,23 @@
     nchunk = tx // REACH
     groups = (tx + 2 * HALF) // REACH
     f32 = jnp.float32
-    vmem = pl.BlockSpec(memory_space=pltpu.VMEM)
     number = STEPS * (2 + 4 * nchunk) + nsnap * 20
     V = pltpu.VMEM
-    return pl.pallas_call(
+    results = (
+        jax.ShapeDtypeStruct((tx, ty, tz), f32),
+        jax.ShapeDtypeStruct((tx, ty, tz), f32),
+        jax.ShapeDtypeStruct((LAGS, tx, ty, tz), jnp.bfloat16),
+    )
+    far = pl.BlockSpec(memory_space=pltpu.HBM)
+    moved = pl.pallas_call(
         kernel,
-        out_shape=(
-            jax.ShapeDtypeStruct((tx, ty, tz), f32),
-            jax.ShapeDtypeStruct((tx, ty, tz), f32),
-            jax.ShapeDtypeStruct((LAGS, tx, ty, tz), jnp.bfloat16),
-        ),
-        in_specs=[pl.BlockSpec(memory_space=pltpu.HBM)] * 10,
-        out_specs=(vmem, vmem, vmem),
+        out_shape=results,
+        in_specs=[far] * 10,
+        out_specs=(far, far, far),
         scratch_shapes=[
+            V((tx, ty, tz), f32),
+            V((tx, ty, tz), f32),
+            V((LAGS, tx, ty, tz), jnp.bfloat16),
             V((STEPS + 2, tx + 2 * H, 8, tz), f32),
             V((STEPS, tx, 8, tz), f32),
             V((STEPS, tx, 8, tz), f32),
@@ -477,6 +519,7 @@
             pltpu.SemaphoreType.DMA((number,)),
             pltpu.SemaphoreType.DMA((number,)),
             pltpu.SemaphoreType.DMA((10,)),
+            pltpu.SemaphoreType.DMA((LAGS + 2,)),
         ],
         compiler_params=pltpu.CompilerParams(
             collective_id=0, has_side_effects=True, vmem_limit_bytes=63 * 2**20
@@ -493,6 +536,14 @@
         receiver_cells.T,
         traces,
     )
+    return pl.pallas_call(
+        deliver,
+        out_shape=results,
+        in_specs=[far] * 3,
+        out_specs=(far, far, far),
+        scratch_shapes=[pltpu.SemaphoreType.DMA((6,))],
+        compiler_params=pltpu.CompilerParams(vmem_limit_bytes=63 * 2**20),
+    )(*moved)
 
 
 def solution(mesh):

time: 39.4 us -> 64.5 us (1.64)
  Pallas kernels: 34 us -> 63.7 us
  local copies, waits for them, and re-layouts: 4.52 us -> 0 us
    pallas_call x1 -> x2, Pallas kernels: 34 us -> 63.7 us  [the longest x1 32.8 us: local(): pl.pallas_call(kernel, out_shape=results, in_specs=[far] * 10, out_specs=...]
    unnamed x5 -> x0, local copies, waits for them, and re-layouts: 4.52 us -> none
where the time goes in v4:
time: 64.5 us; the launch traced here: 64.4 us
  Pallas kernels  63.7 us (99%)
    pallas_call x1, Pallas kernels, local(): pl.pallas_call(kernel, out_shape=results, in_specs=[far] * 10, out_specs=...  32.8 us
    pallas_call x1, Pallas kernels, local(): pl.pallas_call(deliver, out_shape=results, in_specs=[far] * 3, out_specs=...  30.9 us

profile of v4, /device:TPU:0, one launch (start us, length us, event | category | flops | bytes accessed | tf_op | source)
XLA Modules:
  0.0 64.4 jit_solution(1929678681087545696)
XLA Ops:
  0.6 32.8 %shard_map.121 = (f32[12,4,512]{2,1,0:T(4,128)}, f32[12,4,512]{2,1,0:T(4,128)}, bf16[16,12,4,512]{3,2,1,0:T(4,128)(2,1)}) custom-call(f32[12,4,512]{2,1,0:T(4,128)} %sp_in.1, f32[12,4,512]{2,1,0:T(4,128)} %sn_in.1, f32[12,4,512]{2,1,0:T(4,128)} %rp_in.1, f32[12,4,512]{2,1,0:T(4,128)} %rn_in.1, f32[12,4,512]{2,1,0:T(4,128)} %cr_in.1, s32[12,4,512]{2,1,0:T(4,128)} %ab_in.1, ...), custom_call_target="tpu_custom_call" | custom-call | tf_op jit(solution)/shard_map/pallas_call | solution.py:485
  33.4 30.9 %shard_map.122 = (f32[12,4,512]{2,1,0:T(4,128)}, f32[12,4,512]{2,1,0:T(4,128)}, bf16[16,12,4,512]{3,2,1,0:T(4,128)(2,1)}) custom-call(f32[12,4,512]{2,1,0:T(4,128)} %get-tuple-element.6.s, f32[12,4,512]{2,1,0:T(4,128)} %get-tuple-element.7.r, bf16[16,12,4,512]{3,2,1,0:T(4,128)(2,1)} %get-tuple-element.8.i), custom_call_target="tpu_custom_call" | custom-call | tf_op jit(solution)/shard_map/pallas_call | solution.py:539

commit v5 on v4

--- a/solution.py
+++ b/solution.py
@@ -444,16 +444,23 @@
     each(0, LAGS, lambda lag: lag_out(lag).wait())
 
 
-def deliver(s, r, i, out_s, out_r, out_i, sems):
-    pairs = [(s, out_s), (r, out_r)]
-    part = LAGS // 4
-    pairs += [
-        (i.at[k * part : (k + 1) * part], out_i.at[k * part : (k + 1) * part]) for k in range(4)
-    ]
-    moves = [pltpu.make_async_copy(a, b, sems.at[n]) for n, (a, b) in enumerate(pairs)]
-    for c in moves:
+PARTS = 8
+
+
+def deliver(s, r, i, out_s, out_r, out_i, held_s, held_r, held_i, arrive, leave):
+    triples = [(s, held_s, out_s), (r, held_r, out_r)]
+    part = LAGS // PARTS
+    for k in range(PARTS):
+        lags = pl.ds(k * part, part)
+        triples.append((i.at[lags], held_i.at[lags], out_i.at[lags]))
+    first = [pltpu.make_async_copy(a, b, arrive.at[n]) for n, (a, b, c) in enumerate(triples)]
+    second = [pltpu.make_async_copy(b, c, leave.at[n]) for n, (a, b, c) in enumerate(triples)]
+    for c in first:
         c.start()
-    for c in moves:
+    for one, two in zip(first, second):
+        one.wait()
+        two.start()
+    for c in second:
         c.wait()
 
 
@@ -541,7 +548,13 @@
         out_shape=results,
         in_specs=[far] * 3,
         out_specs=(far, far, far),
-        scratch_shapes=[pltpu.SemaphoreType.DMA((6,))],
+        scratch_shapes=[
+            V((tx, ty, tz), f32),
+            V((tx, ty, tz), f32),
+            V((LAGS, tx, ty, tz), jnp.bfloat16),
+            pltpu.SemaphoreType.DMA((PARTS + 2,)),
+            pltpu.SemaphoreType.DMA((PARTS + 2,)),
+        ],
         compiler_params=pltpu.CompilerParams(vmem_limit_bytes=63 * 2**20),
     )(*moved)
 

time: 64.5 us -> 35.7 us (0.55)
  Pallas kernels: 63.7 us -> 34.9 us
    pallas_call x1, Pallas kernels: 30.9 us -> 2.1 us  [local(): pl.pallas_call(deliver, out_shape=results, in_specs=[far] * 3, out_specs=...]
where the time goes in v5:
time: 35.7 us; the launch traced here: 35.5 us
  Pallas kernels  34.9 us (98%)
  between operations  0.64 us (2%)
    pallas_call x1, Pallas kernels, local(): pl.pallas_call(kernel, out_shape=results, in_specs=[far] * 10, out_specs=...  32.8 us
    pallas_call x1, Pallas kernels, local(): pl.pallas_call(deliver, out_shape=results, in_specs=[far] * 3, out_specs=...  2.1 us

profile of v5, /device:TPU:0, one launch (start us, length us, event | category | flops | bytes accessed | tf_op | source)
XLA Modules:
  0.0 35.5 jit_solution(14657658739370813697)
XLA Ops:
  0.6 32.8 %shard_map.121 = (f32[12,4,512]{2,1,0:T(4,128)}, f32[12,4,512]{2,1,0:T(4,128)}, bf16[16,12,4,512]{3,2,1,0:T(4,128)(2,1)}) custom-call(f32[12,4,512]{2,1,0:T(4,128)} %sp_in.1, f32[12,4,512]{2,1,0:T(4,128)} %sn_in.1, f32[12,4,512]{2,1,0:T(4,128)} %rp_in.1, f32[12,4,512]{2,1,0:T(4,128)} %rn_in.1, f32[12,4,512]{2,1,0:T(4,128)} %cr_in.1, s32[12,4,512]{2,1,0:T(4,128)} %ab_in.1, ...), custom_call_target="tpu_custom_call" | custom-call | tf_op jit(solution)/shard_map/pallas_call | solution.py:492
  33.4 2.1 %shard_map.122 = (f32[12,4,512]{2,1,0:T(4,128)}, f32[12,4,512]{2,1,0:T(4,128)}, bf16[16,12,4,512]{3,2,1,0:T(4,128)(2,1)}) custom-call(f32[12,4,512]{2,1,0:T(4,128)} %get-tuple-element.6.s, f32[12,4,512]{2,1,0:T(4,128)} %get-tuple-element.7.r, bf16[16,12,4,512]{3,2,1,0:T(4,128)(2,1)} %get-tuple-element.8.i), custom_call_target="tpu_custom_call" | custom-call | tf_op jit(solution)/shard_map/pallas_call | solution.py:546

commit v6 on v5

--- a/solution.py
+++ b/solution.py
@@ -136,18 +136,22 @@
     each(0, tx, load_now, unroll=4)
     pl.semaphore_wait(barrier, count)
 
-    def send_x(f, low, high):
-        left = Copy(
+    def send_left(f, low, high):
+        return Copy(
             F.at[f, H + low : H + high],
             F.at[f, H + tx + low : H + tx + high],
             (-1, 0, 0),
         )
-        right = Copy(
+
+    def send_right(f, low, high):
+        return Copy(
             F.at[f, H + tx - high : H + tx - low],
             F.at[f, H - high : H - low],
             (1, 0, 0),
         )
-        return left, right
+
+    def send_x(f, low, high):
+        return send_left(f, low, high), send_right(f, low, high)
 
     def send_x_chunk(f, c):
         done = []
@@ -280,13 +284,14 @@
         return jnp.where(parity == 0, pltpu.roll(v, 7, 0), pltpu.roll(v, 1, 0))
 
     def prepare(s, f):
+        def swapped(x):
+            G[s, x] = swap(F[f, x])
+
+        each(H, H + tx, swapped, unroll=6)
         for w in late[s]:
             w.wait()
-
-        def swapped(x):
-            G[s, x] = swap(F[f, x])
-
-        each(0, tx + 2 * H, swapped, unroll=5)
+        each(0, H, swapped, unroll=H)
+        each(H + tx, 2 * H + tx, swapped, unroll=H)
 
         def edges(x):
             edge = jnp.where(lane < LANES // 2, ZR[f - 1, x], ZL[f - 1, x])
@@ -359,14 +364,14 @@
             if not last:
                 yw[nf, c] = send_y(nf, c)
                 zw[nf, c] = send_z(nf, c * REACH, (c + 1) * REACH)
-                if number == min(1, nchunk - 1):
-                    xw[nf] = send_x(nf, 0, REACH)
+                if c == 0:
+                    to_left = send_left(nf, 0, REACH)
+                if c == nchunk - 1:
+                    xw[nf] = to_left, send_right(nf, 0, REACH)
             elif nf in snaps:
                 waits = late.setdefault(snaps.index(nf), [])
                 waits += send_x_chunk(nf, c)
                 waits += send_rows(nf, snaps.index(nf), c)
-            if f in snaps:
-                late[snaps.index(f)] += relay_rows(f, snaps.index(f), c)
         if nf in snaps:
             s = snaps.index(nf)
             waits = late.setdefault(s, [])
@@ -376,6 +381,9 @@
                 waits += send_z(nf, 0, tx)
             waits += send_z(nf, 0, HALF, -1)
             waits += send_z(nf, tx - HALF, tx, 1)
+        if f in snaps:
+            for g in range(nchunk):
+                late[snaps.index(f)] += relay_rows(f, snaps.index(f), g)
 
     def out_fields(x):
         out_s[x], out_r[x] = unweave(x, F[STEPS + 1, H + x], (even, odd))

time: 35.7 us -> 35.5 us (level)
  no operation moved by 1% of the time
where the time goes in v6:
time: 35.5 us; the launch traced here: 35.3 us
  Pallas kernels  34.7 us (98%)
  between operations  0.64 us (2%)
    pallas_call x1, Pallas kernels, local(): pl.pallas_call(kernel, out_shape=results, in_specs=[far] * 10, out_specs=...  32.6 us
    pallas_call x1, Pallas kernels, local(): pl.pallas_call(deliver, out_shape=results, in_specs=[far] * 3, out_specs=...  2.1 us

profile of v6, /device:TPU:0, one launch (start us, length us, event | category | flops | bytes accessed | tf_op | source)
XLA Modules:
  0.0 35.3 jit_solution(11883826664527179941)
XLA Ops:
  0.6 32.6 %shard_map.121 = (f32[12,4,512]{2,1,0:T(4,128)}, f32[12,4,512]{2,1,0:T(4,128)}, bf16[16,12,4,512]{3,2,1,0:T(4,128)(2,1)}) custom-call(f32[12,4,512]{2,1,0:T(4,128)} %sp_in.1, f32[12,4,512]{2,1,0:T(4,128)} %sn_in.1, f32[12,4,512]{2,1,0:T(4,128)} %rp_in.1, f32[12,4,512]{2,1,0:T(4,128)} %rn_in.1, f32[12,4,512]{2,1,0:T(4,128)} %cr_in.1, s32[12,4,512]{2,1,0:T(4,128)} %ab_in.1, ...), custom_call_target="tpu_custom_call" | custom-call | tf_op jit(solution)/shard_map/pallas_call | solution.py:500
  33.2 2.1 %shard_map.122 = (f32[12,4,512]{2,1,0:T(4,128)}, f32[12,4,512]{2,1,0:T(4,128)}, bf16[16,12,4,512]{3,2,1,0:T(4,128)(2,1)}) custom-call(f32[12,4,512]{2,1,0:T(4,128)} %get-tuple-element.6.s, f32[12,4,512]{2,1,0:T(4,128)} %get-tuple-element.7.r, bf16[16,12,4,512]{3,2,1,0:T(4,128)(2,1)} %get-tuple-element.8.i), custom_call_target="tpu_custom_call" | custom-call | tf_op jit(solution)/shard_map/pallas_call | solution.py:554

commit v7 on v6

--- a/solution.py
+++ b/solution.py
@@ -133,7 +133,7 @@
         c.start()
     for c in fetched[:2]:
         c.wait()
-    each(0, tx, load_now, unroll=4)
+    each(0, REACH, load_now, unroll=REACH)
     pl.semaphore_wait(barrier, count)
 
     def send_left(f, low, high):
@@ -224,10 +224,15 @@
 
     order = [0] + [nchunk - 1] * (nchunk > 1) + list(range(1, nchunk - 1))
     xw, yw, zw = {}, {}, {}
-    xw[1] = send_x(1, 0, REACH)
     for c in order:
+        if c:
+            each(c * REACH, (c + 1) * REACH, load_now, unroll=REACH)
         yw[1, c] = send_y(1, c)
         zw[1, c] = send_z(1, c * REACH, (c + 1) * REACH)
+        if c == 0:
+            to_left = send_left(1, 0, REACH)
+        if c == nchunk - 1:
+            xw[1] = to_left, send_right(1, 0, REACH)
 
     def zero(missing, *refs):
         @pl.when(missing)

time: 35.5 us -> 35.5 us (level)
  no operation moved by 1% of the time
where the time goes in v7:
time: 35.5 us; the launch traced here: 35.3 us
  Pallas kernels  34.7 us (98%)
  between operations  0.64 us (2%)
    pallas_call x1, Pallas kernels, local(): pl.pallas_call(kernel, out_shape=results, in_specs=[far] * 10, out_specs=...  32.6 us
    pallas_call x1, Pallas kernels, local(): pl.pallas_call(deliver, out_shape=results, in_specs=[far] * 3, out_specs=...  2.1 us

profile of v7, /device:TPU:0, one launch (start us, length us, event | category | flops | bytes accessed | tf_op | source)
XLA Modules:
  0.0 35.3 jit_solution(6594366440417986162)
XLA Ops:
  0.6 32.6 %shard_map.121 = (f32[12,4,512]{2,1,0:T(4,128)}, f32[12,4,512]{2,1,0:T(4,128)}, bf16[16,12,4,512]{3,2,1,0:T(4,128)(2,1)}) custom-call(f32[12,4,512]{2,1,0:T(4,128)} %sp_in.1, f32[12,4,512]{2,1,0:T(4,128)} %sn_in.1, f32[12,4,512]{2,1,0:T(4,128)} %rp_in.1, f32[12,4,512]{2,1,0:T(4,128)} %rn_in.1, f32[12,4,512]{2,1,0:T(4,128)} %cr_in.1, s32[12,4,512]{2,1,0:T(4,128)} %ab_in.1, ...), custom_call_target="tpu_custom_call" | custom-call | tf_op jit(solution)/shard_map/pallas_call | solution.py:505
  33.2 2.1 %shard_map.122 = (f32[12,4,512]{2,1,0:T(4,128)}, f32[12,4,512]{2,1,0:T(4,128)}, bf16[16,12,4,512]{3,2,1,0:T(4,128)(2,1)}) custom-call(f32[12,4,512]{2,1,0:T(4,128)} %get-tuple-element.6.s, f32[12,4,512]{2,1,0:T(4,128)} %get-tuple-element.7.r, bf16[16,12,4,512]{3,2,1,0:T(4,128)(2,1)} %get-tuple-element.8.i), custom_call_target="tpu_custom_call" | custom-call | tf_op jit(solution)/shard_map/pallas_call | solution.py:559
